TPU v7x, 128 devices: a whole 4x4x4 slice. The times are simulated.
128 devices in a mesh: dp: 16 (over x, y), ep: 8 (over z, core).
Axes of the slice: x: 4, y: 4, z: 4, core: 2. Of those that a mesh axis runs over, the one named last changes fastest.
Arguments:
- queries: bfloat16 [4096, 64, 576], P('dp', 'ep'), may hold values from -24 to 24
- prefix_latents: bfloat16 [16, 2048, 576], P('dp', 'ep'), may hold values from -6 to 6
- new_latents: bfloat16 [16, 256, 576], P('dp', 'ep'), may hold values from -6 to 6
- prefix_lengths: int32 [16], replicated, may hold values from 2 to 2048, as said below
- span_sources: int32 [16], replicated, may hold values from 0 to 15, as said below
- value_up: bfloat16 [64, 512, 128], P('ep'), may hold values from -0.25 to 0.25
- out_proj: bfloat16 [8192, 3584], P('ep', 'dp'), may hold values from -0.5 to 0.5
- residual: bfloat16 [4096, 3584], P(('dp', 'ep')), may hold values from -54 to 54
- norm_gain: bfloat16 [3584], replicated, may hold values from 0.099609375 to 1.8984375
- expert_gate: bfloat16 [128, 3584, 1024], P(('dp', 'ep')), may hold values from -0.09375 to 0.09375
- expert_up: bfloat16 [128, 3584, 1024], P(('dp', 'ep')), may hold values from -0.09375 to 0.09375
- expert_down: bfloat16 [128, 1024, 3584], P(('dp', 'ep')), may hold values from -0.1875 to 0.1875
- expert_ids: int32 [4096, 8], P(('dp', 'ep')), may hold values from 0 to 127, all different within a row; in each aligned block of 32 rows (0 to 31, 32 to 63, ...) at most 2 rows name the same one
- gate_weights: float32 [4096, 8], P(('dp', 'ep')), may hold values from 0.05 to 0.5
- decode_owner: int32 [16], replicated, may hold values from 0 to 15, each once
Outputs:
- layer_out: bfloat16 [4096, 3584], P(('dp', 'ep'))
- decode_latents: bfloat16 [16, 256, 576], P('dp', 'ep')
Inputs may be any that keep to these rules, and one draw needn't show every extreme that they name: `prefix_lengths`: one prompt has all 2048 cached positions valid. `span_sources`: a permutation of the prompts. `expert_ids`: each row names 8 different experts; among the rows of one device (aligned blocks of 32 rows) no expert is named by more than 2 rows, and in some blocks one expert is named by exactly 2. `decode_owner`: a permutation of the prompts; slot o of decode_latents lives on index o of dp.
All inputs are finite; a program needn't handle non-finite values.
Results may differ from a plain program's by a relative error of at most 0.017.
Values may be sent and summed in bfloat16 or wider, within the bound.
A program may use at most 192 MiB of HBM per device.

v0:
```python
import functools

import jax
import jax.numpy as jnp
from jax import lax
from jax.experimental import pallas as pl
from jax.experimental.pallas import tpu as pltpu
from jax.sharding import PartitionSpec as P

TOP = 8


score_scale = 192.0 ** (-0.5)
norm_eps = 1e-06


def attend(queries, keys, length, positions, prefix_len, latent_width):
    prefix_all = keys[:prefix_len]
    new_all = keys[prefix_len:]
    scores_old = (
        jnp.einsum("thc,jc->thj", queries, prefix_all, preferred_element_type=jnp.float32)
        * score_scale
    )
    scores_new = (
        jnp.einsum("thc,jc->thj", queries, new_all, preferred_element_type=jnp.float32)
        * score_scale
    )
    old_pos = lax.broadcasted_iota(jnp.int32, scores_old.shape, 2)
    old_valid = old_pos < length
    new_pos = lax.broadcasted_iota(jnp.int32, scores_new.shape, 2)
    new_valid = new_pos <= positions[:, None, None]
    scores_old = jnp.where(old_valid, scores_old, -1e30)
    scores_new = jnp.where(new_valid, scores_new, -1e30)
    row_max = jnp.maximum(jnp.max(scores_old, axis=2), jnp.max(scores_new, axis=2))[:, :, None]
    exp_old = jnp.where(old_valid, jnp.exp(scores_old - row_max), 0.0)
    exp_new = jnp.where(new_valid, jnp.exp(scores_new - row_max), 0.0)
    weight_sum = jnp.sum(exp_old, axis=2) + jnp.sum(exp_new, axis=2)
    weighted = jnp.einsum(
        "thj,jl->thl",
        exp_old.astype(jnp.bfloat16),
        prefix_all[:, :latent_width],
        preferred_element_type=jnp.float32,
    )
    weighted = weighted + jnp.einsum(
        "thj,jl->thl",
        exp_new.astype(jnp.bfloat16),
        new_all[:, :latent_width],
        preferred_element_type=jnp.float32,
    )
    return (weighted / weight_sum[:, :, None]).astype(jnp.bfloat16)


MESH = pl.DeviceIdType.MESH


def partners(count, me, each):
    def step(k, carry):
        each(lax.rem(me + k, count))
        return carry

    lax.fori_loop(1, count, step, 0)


def block_rows(start, size):
    return pl.ds(pl.multiple_of(start * size, size), size)


def moe_kernel(
    sizes,
    att_ref,
    res_ref,
    gain_ref,
    ids_ref,
    ids_t_ref,
    gates_ref,
    gate_hbm,
    up_hbm,
    down_hbm,
    out_ref,
    w_gate,
    w_up,
    w_down,
    hid,
    s1,
    r1,
    s2,
    r2,
    total,
    act,
    o1,
    q1,
    q2,
    q3,
    send_sems,
    recv_sems,
    weight_sems,
):
    n_dp, n_ep, chunks = sizes
    dp, ep = lax.axis_index("dp"), lax.axis_index("ep")
    rows = n_dp * n_ep * 2
    dp_block, ep_block = 2 * n_ep, 2 * n_dp
    cols = hid.shape[1] // chunks
    tokens = hid.shape[0]
    hidden_units = w_gate.shape[1]

    loads = [
        pltpu.make_async_copy(src.at[0], dst, weight_sems.at[i])
        for i, (src, dst) in enumerate(((gate_hbm, w_gate), (up_hbm, w_up), (down_hbm, w_down)))
    ]
    for load in loads:
        load.start()

    barrier = pltpu.get_barrier_semaphore()
    partners(
        n_dp,
        dp,
        lambda p: pl.semaphore_signal(barrier, inc=1, device_id=(p, ep), device_id_type=MESH),
    )
    partners(
        n_ep,
        ep,
        lambda p: pl.semaphore_signal(barrier, inc=1, device_id=(dp, p), device_id_type=MESH),
    )

    def send_dp(stage, c, src, dst):
        def each(p):
            pltpu.make_async_remote_copy(
                src_ref=src.at[c, block_rows(p, dp_block)],
                dst_ref=dst.at[c, block_rows(dp, dp_block)],
                send_sem=send_sems.at[stage, c],
                recv_sem=recv_sems.at[stage, c],
                device_id=(p, ep),
                device_id_type=MESH,
            ).start()

        partners(n_dp, dp, each)
        dst[c, block_rows(dp, dp_block)] = src[c, block_rows(dp, dp_block)]

    def send_ep(stage, c, src, dst):
        def each(p):
            pltpu.make_async_remote_copy(
                src_ref=src.at[c, block_rows(p, ep_block)],
                dst_ref=dst.at[c, block_rows(ep, ep_block)],
                send_sem=send_sems.at[stage, c],
                recv_sem=recv_sems.at[stage, c],
                device_id=(dp, p),
                device_id_type=MESH,
            ).start()

        partners(n_ep, ep, each)
        dst[c, block_rows(ep, ep_block)] = src[c, block_rows(ep, ep_block)]

    def wait_all(sems, stage, c, ref):
        size = rows - (dp_block if stage in (0, 3) else ep_block)
        part = ref.at[c, pl.ds(0, size)]
        pltpu.make_async_copy(part, part, sems.at[stage, c]).wait()

    def mm(a, b):
        return jnp.dot(a, b, preferred_element_type=jnp.float32)

    slot_col = lax.broadcasted_iota(jnp.int32, (rows, tokens), 0)
    slot_row = lax.broadcasted_iota(jnp.int32, (tokens, rows), 1)
    named_t = jnp.zeros((rows, tokens), jnp.float32)
    named = jnp.zeros((tokens, rows), jnp.float32)
    weight = jnp.zeros((tokens, rows), jnp.float32)
    for k in range(TOP):
        named_t += jnp.where(ids_t_ref[k : k + 1, :] == (slot_col >> 1), 1.0, 0.0)
        hit = ids_ref[:, k : k + 1] == (slot_row >> 1)
        named += jnp.where(hit, 1.0, 0.0)
        weight += jnp.where(hit, gates_ref[:, k : k + 1], 0.0)
    first = lax.broadcasted_iota(jnp.int32, (tokens, tokens), 0)
    second = lax.broadcasted_iota(jnp.int32, (tokens, tokens), 1)
    before_t = jnp.where(first < second, 1.0, 0.0).astype(jnp.bfloat16)
    before = jnp.where(second < first, 1.0, 0.0).astype(jnp.bfloat16)
    rank_t = mm(named_t.astype(jnp.bfloat16), before_t)
    rank = mm(before, named.astype(jnp.bfloat16))
    pick = jnp.where(rank_t == (slot_col & 1).astype(jnp.float32), named_t, 0.0).astype(
        jnp.bfloat16
    )
    weight = jnp.where(rank == (slot_row & 1).astype(jnp.float32), weight, 0.0)
    weight_high = weight.astype(jnp.bfloat16)
    weight_low = (weight - weight_high.astype(jnp.float32)).astype(jnp.bfloat16)
    weights = jnp.concatenate([weight_high, weight_low], axis=0)
    to = lax.broadcasted_iota(jnp.int32, (rows, rows), 0)
    frm = lax.broadcasted_iota(jnp.int32, (rows, rows), 1)
    by_ep = lax.rem(to >> 1, n_dp) * dp_block + (to // ep_block) * 2 + (to & 1)
    by_dp = lax.rem(to >> 1, n_ep) * ep_block + (to // dp_block) * 2 + (to & 1)
    perm_ep = jnp.where(frm == by_ep, 1.0, 0.0).astype(jnp.bfloat16)
    perm_dp = jnp.where(frm == by_dp, 1.0, 0.0).astype(jnp.bfloat16)

    hidden = res_ref[...].astype(jnp.float32) + att_ref[...].astype(jnp.float32)
    hid[...] = hidden
    mean_square = jnp.mean(hidden * hidden, axis=1, keepdims=True)
    scale = lax.rsqrt(mean_square + norm_eps)

    pl.semaphore_wait(barrier, n_dp + n_ep - 2)

    for c in range(chunks):
        span = pl.ds(c * cols, cols)
        normed = (hid[:, span] * scale * gain_ref[:, span].astype(jnp.float32)).astype(
            jnp.bfloat16
        )
        s1[c] = mm(pick, normed).astype(jnp.bfloat16)
        send_dp(0, c, s1, r1)
    for c in range(chunks):
        wait_all(recv_sems, 0, c, r1)
        s2[c] = mm(perm_ep, r1[c]).astype(jnp.bfloat16)
        send_ep(1, c, s2, r2)
    loads[0].wait()
    loads[1].wait()
    for c in range(chunks):
        wait_all(recv_sems, 1, c, r2)
        span = pl.ds(c * cols, cols)
        x = r2[c]
        gate_part = mm(x, w_gate[span, :])
        up_part = mm(x, w_up[span, :])
        if c:
            gate_part += total[:, pl.ds(0, hidden_units)]
            up_part += total[:, pl.ds(hidden_units, hidden_units)]
        if c < chunks - 1:
            total[:, pl.ds(0, hidden_units)] = gate_part
            total[:, pl.ds(hidden_units, hidden_units)] = up_part
        else:
            act[...] = (gate_part / (1.0 + jnp.exp(-gate_part)) * up_part).astype(jnp.bfloat16)
    loads[2].wait()
    for c in range(chunks):
        o1[c] = mm(act[...], w_down[:, pl.ds(c * cols, cols)]).astype(jnp.bfloat16)
        send_ep(2, c, o1, q1)
    for c in range(chunks):
        wait_all(recv_sems, 2, c, q1)
        q2[c] = mm(perm_dp, q1[c]).astype(jnp.bfloat16)
        send_dp(3, c, q2, q3)
    for c in range(chunks):
        wait_all(recv_sems, 3, c, q3)
        span = pl.ds(c * cols, cols)
        both = mm(weights, q3[c])
        out_ref[:, span] = (hid[:, span] + (both[:tokens] + both[tokens:])).astype(out_ref.dtype)
    for stage, ref in enumerate((s1, s2, o1, q2)):
        for c in range(chunks):
            wait_all(send_sems, stage, c, ref)


def moe(attention, residual, norm_gain, expert_ids, gate_weights, expert_gate, expert_up, expert_down):
    n_dp, n_ep = lax.axis_size("dp"), lax.axis_size("ep")
    tokens, width = residual.shape
    units = expert_gate.shape[2]
    rows = n_dp * n_ep * 2
    chunks = 4
    buf = pltpu.VMEM((chunks, rows, width // chunks), jnp.bfloat16)
    vmem = pl.BlockSpec(memory_space=pltpu.VMEM)
    hbm = pl.BlockSpec(memory_space=pl.ANY)
    return pl.pallas_call(
        functools.partial(moe_kernel, (n_dp, n_ep, chunks)),
        out_shape=jax.ShapeDtypeStruct((tokens, width), jnp.bfloat16),
        in_specs=[vmem] * 6 + [hbm] * 3,
        out_specs=vmem,
        scratch_shapes=[
            pltpu.VMEM((width, units), jnp.bfloat16),
            pltpu.VMEM((width, units), jnp.bfloat16),
            pltpu.VMEM((units, width), jnp.bfloat16),
            pltpu.VMEM((tokens, width), jnp.float32),
            buf,
            buf,
            buf,
            buf,
            pltpu.VMEM((rows, 2 * units), jnp.float32),
            pltpu.VMEM((rows, units), jnp.bfloat16),
            buf,
            buf,
            buf,
            buf,
            pltpu.SemaphoreType.DMA((4, chunks)),
            pltpu.SemaphoreType.DMA((4, chunks)),
            pltpu.SemaphoreType.DMA((3,)),
        ],
        compiler_params=pltpu.CompilerParams(
            collective_id=1, has_side_effects=True, vmem_limit_bytes=60 * 2**20
        ),
        name="experts",
    )(
        attention,
        residual,
        norm_gain.reshape(1, -1),
        expert_ids,
        expert_ids.T,
        gate_weights,
        expert_gate,
        expert_up,
        expert_down,
    )


def shards(
    queries,
    prefix_latents,
    new_latents,
    prefix_lengths,
    span_sources,
    value_up,
    out_proj,
    residual,
    norm_gain,
    expert_gate,
    expert_up,
    expert_down,
    expert_ids,
    gate_weights,
    decode_owner,
):
    latent_width = value_up.shape[1]
    model_width = residual.shape[1]
    dp_count = lax.axis_size("dp")
    ep_count = lax.axis_size("ep")
    slot = lax.axis_index("dp")
    span_len = queries.shape[0]
    key_width = queries.shape[2]
    late_rows = span_len // 4
    home_rows = span_len - late_rows
    prefix_part = prefix_latents.shape[1]
    prefix_len = prefix_part * ep_count
    prefix_all, new_all = (
        lax.all_gather(prefix_latents, "ep", axis=1, tiled=True),
        lax.all_gather(new_latents, "ep", axis=1, tiled=True),
    )
    own_keys = jnp.concatenate([prefix_all[0], new_all[0]], axis=0)
    positions = jnp.arange(span_len, dtype=jnp.int32)
    source = span_sources[slot]
    slot_ids = jnp.arange(dp_count, dtype=jnp.int32)
    own_length = prefix_lengths[slot]
    first = attend(
        queries[:home_rows], own_keys, own_length, positions[:home_rows], prefix_len, latent_width
    )
    pieces = jnp.concatenate(
        [
            prefix_latents.reshape(dp_count, -1, key_width),
            new_latents.reshape(dp_count, -1, key_width),
        ],
        axis=1,
    )
    old_rows = prefix_part // dp_count
    spread = lax.all_to_all(pieces, "dp", split_axis=0, concat_axis=0, tiled=True)
    given = jnp.zeros_like(decode_owner).at[decode_owner].set(slot_ids)
    routed = jnp.concatenate([spread[span_sources], spread[given][:, old_rows:]], axis=1)
    arrived = lax.all_to_all(routed, "dp", split_axis=0, concat_axis=0, tiled=True)
    piece_rows = pieces.shape[1]
    moved_shard = jnp.concatenate(
        [
            arrived[:, :old_rows].reshape(-1, key_width),
            arrived[:, old_rows:piece_rows].reshape(-1, key_width),
        ],
        axis=0,
    )
    decode_latents = arrived[:, piece_rows:].reshape(new_latents.shape)
    moved_prefix, moved_new = (
        lax.all_gather(moved_shard[:prefix_part], "ep", axis=0, tiled=True),
        lax.all_gather(moved_shard[prefix_part:], "ep", axis=0, tiled=True),
    )
    moved_keys = jnp.concatenate([moved_prefix, moved_new], axis=0)
    last = attend(
        queries[home_rows:],
        moved_keys,
        prefix_lengths[source],
        positions[home_rows:],
        prefix_len,
        latent_width,
    )
    latent_out = jnp.concatenate([first, last], axis=0)
    head_rows = jnp.einsum(
        "thl,hlv->thv", latent_out, value_up, preferred_element_type=jnp.float32
    ).astype(jnp.bfloat16)
    head_rows = head_rows.reshape(span_len, -1)
    projected = jnp.dot(
        head_rows,
        lax.all_gather(out_proj, "dp", axis=1, tiled=True),
        preferred_element_type=jnp.float32,
    )
    attention = lax.psum_scatter(
        projected.astype(jnp.bfloat16), "ep", scatter_dimension=0, tiled=True
    )
    layer_out = moe(
        attention,
        residual,
        norm_gain,
        expert_ids,
        gate_weights,
        expert_gate,
        expert_up,
        expert_down,
    )
    return (layer_out, decode_latents)


def solution(mesh):
    return jax.shard_map(
        shards,
        mesh=mesh,
        in_specs=(
            P("dp", "ep", None),
            P("dp", "ep", None),
            P("dp", "ep", None),
            P(),
            P(),
            P("ep", None, None),
            P("ep", "dp"),
            P(("dp", "ep"), None),
            P(),
            P(("dp", "ep"), None, None),
            P(("dp", "ep"), None, None),
            P(("dp", "ep"), None, None),
            P(("dp", "ep"), None),
            P(("dp", "ep"), None),
            P(),
        ),
        out_specs=(P(("dp", "ep"), None), P("dp", "ep", None)),
        check_vma=False,
    )
```

profile of v0, /device:TPU:1, one launch (start us, length us, event | category | flops | bytes accessed | tf_op | source)
XLA Modules:
  0.0 265.2 jit_solution(10796990448499699775)
XLA Ops:
  7.2 0.7 all-gather.4.cloned.1.call-update
  7.9 1.2 copy.41
  9.1 0.8 reshape.48
  9.9 0.8 pad_maximum_fusion
  10.7 7.6 %all-to-all-start = ((bf16[16,18,576]{2,1,0:T(8,128)(2,1)}), bf16[16,18,576]{2,1,0:T(8,128)(2,1)S(1)}, u32[]{:S(2)}, u32[]{:S(2)}) async-start(bf16[16,18,576]{2,1,0:T(8,128)(2,1)} %pad_maximum_fusion), calls=%async_computation | async-start | bytes 983040 | tf_op jit(solution)/shard_map/all_to_all | solution.py:341
  18.4 0.7 compare_select_fusion.1
  19.0 0.6 scatter_custom_fusion
  19.7 0.7 compare_select_fusion.2
  20.4 7.9 %all-to-all-done = bf16[16,18,576]{2,1,0:T(8,128)(2,1)S(1)} async-done(((bf16[16,18,576]{2,1,0:T(8,128)(2,1)}), bf16[16,18,576]{2,1,0:T(8,128)(2,1)S(1)}, u32[]{:S(2)}, u32[]{:S(2)}) %all-to-all-start) | async-done | bytes 331808 | tf_op jit(solution)/shard_map/all_to_all | solution.py:341
  28.3 0.6 gather_fusion.1
  29.0 1.4 gather_fusion
  30.3 1.3 pad_maximum_fusion.1
  31.6 12.2 %all_to_all.10 = bf16[16,20,576]{2,1,0:T(8,128)(2,1)S(1)} all-to-all(bf16[16,20,576]{2,1,0:T(8,128)(2,1)S(1)} %pad_maximum_fusion.1), channel_id=1, replica_groups=mesh['dp'=16,'ep'=8] {'dp'}, dimensions={0} | all-to-all | bytes 737280 | tf_op jit(solution)/shard_map/all_to_all | solution.py:344
  43.8 0.8 copy-done.2
  44.6 0.8 slice.59
  45.4 1.8 copy.42
  47.3 0.7 all-gather.8.cloned.1.call-update
  49.9 3.4 %copy.55 = bf16[192,8,576]{2,1,0:T(8,128)(2,1)} copy(bf16[192,8,576]{0,2,1:T(8,128)(2,1)S(1)} %bitcast.67) | data formatting | bytes 3538944
  53.3 18.6 %all_gather.16 = bf16[1,256,576]{2,1,0:T(8,128)(2,1)} all-gather(bf16[1,32,576]{2,1,0:T(8,128)(2,1)S(1)} %copy-done.9), channel_id=1, replica_groups=mesh['dp'=16,'ep'=8] {'ep'}, dimensions={1}, use_global_device_ids=true | all-gather | bytes 331776 | tf_op jit(solution)/shard_map/all_gather | solution.py:323
  71.9 1.8 copy.35
  74.5 0.6 fusion.53
  75.1 0.7 iota_compare_fusion.3
  75.8 0.7 iota_compare_fusion.2
  77.0 4.2 %fusion.55 = (f32[192,8]{1,0:T(8,128)}, f32[192,8,256]{2,1,0:T(8,128)}) fusion(bf16[192,8,576]{2,1,0:T(8,128)(2,1)} %copy.55, bf16[1,256,576]{2,1,0:T(8,128)(2,1)} %all_gather.16, s32[192]{0:T(256)S(1)} %bitcast.72), kind=kOutput, calls=%fused_computation.81 | convolution fusion | flops 454556160 | bytes 3644160 | tf_op jit(solution)/shard_map/thc,jc->thj/dot_general | solution.py:25
  81.2 1.1 fusion.52
  82.3 12.9 %all_gather.18 = bf16[256,576]{1,0:T(8,128)(2,1)S(1)} all-gather(bf16[32,576]{1,0:T(8,128)(2,1)S(1)} %reshape.50), channel_id=1, replica_groups=mesh['dp'=16,'ep'=8] {'ep'}, dimensions={0}, use_global_device_ids=true | all-gather | bytes 331776 | tf_op jit(solution)/shard_map/all_gather | solution.py:356
  95.2 0.7 copy-done.6
  95.9 2.7 %fusion.54 = (f32[64,8]{0,1:T(8,128)}, f32[64,8,256]{2,0,1:T(8,128)}) fusion(bf16[256,8,576]{0,2,1:T(8,128)(2,1)S(1)} %copy-done.1, bf16[256,576]{1,0:T(8,128)(2,1)S(1)} %all_gather.18, s32[64]{0:T(128)S(1)} %slice.47), kind=kOutput, calls=%fused_computation.80 | convolution fusion | flops 151518720 | bytes 2034176 | tf_op jit(solution)/shard_map/thc,jc->thj/dot_general | solution.py:25
  98.6 8.3 %fusion = (f32[192,8]{1,0:T(8,128)S(1)}, f32[192,8,2048]{2,1,0:T(8,128)S(1)}) fusion(pred[2048]{0:T(1024)(128)(4,1)S(1)} %iota_compare_fusion.3, bf16[192,8,576]{2,1,0:T(8,128)(2,1)} %copy.55, bf16[1,2048,576]{1,2,0:T(8,128)(2,1)} %all-gather.4.cloned.1.call-done), kind=kOutput, calls=%fused_computation.5 | convolution fusion | flops 3633314304 | bytes 16719872 | tf_op jit(solution)/shard_map/thc,jc->thj/dot_general | solution.py:21
  107.0 2.1 fusion.33
  109.0 5.1 %fusion.1 = (f32[192,8]{1,0:T(8,128)S(1)}, bf16[192,8,2048]{2,1,0:T(8,128)(2,1)}) fusion(f32[192,8,2048]{2,1,0:T(8,128)S(1)} %get-tuple-element.15, f32[192,8]{1,0:T(8,128)S(1)} %max.14, pred[2048]{0:T(1024)(128)(4,1)S(1)} %iota_compare_fusion.3), kind=kLoop, calls=%fused_computation.6 | loop fusion | flops 18872832 | bytes 18888704 | tf_op jit(solution)/shard_map/reduce_sum | solution.py:37
  114.2 0.7 copy.40
  114.9 11.2 %fusion.3 = f32[192,8,512]{2,0,1:T(8,128)S(1)} fusion(bf16[192,8,2048]{2,1,0:T(8,128)(2,1)} %get-tuple-element.3, bf16[2048,576]{0,1:T(8,128)(2,1)} %bitcast.74), kind=kOutput, calls=%fused_computation.8 | convolution fusion | flops 3221225472 | bytes 11534336 | tf_op jit(solution)/shard_map/thj,jl->thl/dot_general | solution.py:38
  126.1 1.9 divide_convert_fusion
  127.9 4.2 %bitcast_reduce_fusion = (f32[64,8]{0,1:T(8,128)S(1)}, f32[2048,64,8]{0,1,2:T(8,128)S(1)}) fusion(pred[2048]{0:T(1024)(128)(4,1)S(1)} %iota_compare_fusion.2, bf16[256,8,576]{0,2,1:T(8,128)(2,1)S(1)} %copy-done.1, bf16[2048,576]{0,1:T(8,128)(2,1)} %all-gather.6.cloned.1.call-done), kind=kOutput, calls=%fused_computation.12 | convolution fusion | flops 1211104768 | bytes 7737344 | tf_op jit(solution)/shard_map/thc,jc->thj/dot_general | solution.py:21
  132.4 1.1 fusion.7
  133.9 1.4 fusion.13
  135.6 1.1 copy-done.23
  136.7 0.8 fusion.26
  137.5 9.4 %all-gather.8.cloned.1.call-done = bf16[1024,3584]{0,1:T(8,128)(2,1)} async-done(((bf16[1024,224]{0,1:T(8,128)(2,1)}), bf16[1024,3584]{0,1:T(8,128)(2,1)}) %all-gather.8.cloned.1.call-update) | async-done | bytes 7340048 | tf_op jit(solution)/shard_map/all_gather | solution.py:374
  146.9 6.5 %convolution_convert_fusion = bf16[256,3584]{1,0:T(8,128)(2,1)} fusion(bf16[256,1024]{0,1:T(8,128)(2,1)S(1)} %bitcast.75, bf16[1024,3584]{0,1:T(8,128)(2,1)} %all-gather.8.cloned.1.call-done), kind=kOutput, calls=%fused_computation.10 | convolution fusion | flops 1879965696 | bytes 9699328 | tf_op jit(solution)/shard_map/dot_general | solution.py:372
  153.5 0.7 copy.46.ids_ref
  154.2 0.7 copy.47.gates_ref
  154.9 0.6 reshape.52.gain_ref
  155.5 0.7 reshape.53
  156.1 27.5 %reduce-scatter.2.cloned.1.call-done.att_ref = bf16[32,3584]{1,0:T(8,128)(2,1)} async-done(((bf16[256,3584]{1,0:T(8,128)(2,1)}), bf16[32,3584]{1,0:T(8,128)(2,1)}) %reduce-scatter.2.cloned.1.call-update) | async-done | bytes 229392 | tf_op jit(solution)/shard_map/reduce_scatter | solution.py:377
  183.6 73.4 %experts.1 = bf16[32,3584]{1,0:T(8,128)(2,1)} custom-call(bf16[32,3584]{1,0:T(8,128)(2,1)} %reduce-scatter.2.cloned.1.call-done.att_ref, bf16[32,3584]{1,0:T(8,128)(2,1)} %res_ref.1, bf16[1,3584]{1,0:T(2,128)(2,1)} %reshape.52.gain_ref, s32[32,8]{1,0:T(8,128)} %copy.46.ids_ref, s32[8,32]{1,0:T(8,128)} %bitcast.71, f32[32,8]{1,0:T(8,128)} %copy.47.gates_ref, ...), custom_call_target="tpu_custom_call" | custom-call | tf_op jit(solution)/shard_map/experts/pallas_call | solution.py:252
  257.1 1.6 copy.62
  (69 shorter events, 2.6 us)
Async XLA Ops:
  7.2 128.5 %copy-start = (bf16[8,512,128]{2,1,0:T(8,128)(2,1)S(1)}, bf16[8,512,128]{2,1,0:T(8,128)(2,1)}, u32[]{:S(2)}) copy-start(bf16[8,512,128]{2,1,0:T(8,128)(2,1)} %param.20) | copy-start | bytes 3145732
  7.2 91.4 %all-gather.4.cloned.1.call-start = ((), (), s32[]{:S(2)}) async-start(), calls=%async_computation.3 | async-start | bytes 2654208 | tf_op jit(solution)/shard_map/all_gather | solution.py:322
  10.7 17.6 %all-to-all-start = ((bf16[16,18,576]{2,1,0:T(8,128)(2,1)}), bf16[16,18,576]{2,1,0:T(8,128)(2,1)S(1)}, u32[]{:S(2)}, u32[]{:S(2)}) async-start(bf16[16,18,576]{2,1,0:T(8,128)(2,1)} %pad_maximum_fusion), calls=%async_computation | async-start | bytes 983040 | tf_op jit(solution)/shard_map/all_to_all | solution.py:341
  18.3 29.7 %copy-start.22 = (s32[16]{0:T(128)S(1)}, s32[16]{0:T(128)}, u32[]{:S(2)}) copy-start(s32[16]{0:T(128)} %param.19) | copy-start | bytes 196
  18.3 109.6 %all-gather.6.cloned.1.call-start = ((), (), s32[]{:S(2)}) async-start(), calls=%async_computation.4 | async-start | bytes 2654208 | tf_op jit(solution)/shard_map/all_gather | solution.py:355
  30.3 19.6 %copy-start.1 = (bf16[256,8,576]{0,2,1:T(8,128)(2,1)S(1)}, bf16[256,8,576]{0,2,1:T(8,128)(2,1)}, u32[]{:S(2)}) copy-start(bf16[256,8,576]{0,2,1:T(8,128)(2,1)} %param.15) | copy-start | bytes 7077892
  43.8 0.8 copy-start.2
  44.6 8.7 %copy-start.9 = (bf16[1,32,576]{2,1,0:T(8,128)(2,1)S(1)}, bf16[1,32,576]{2,1,0:T(8,128)(2,1)}, u32[]{:S(2)}) copy-start(bf16[1,32,576]{2,1,0:T(8,128)(2,1)} %param.17) | copy-start | bytes 110596
  47.2 27.3 %copy-start.16 = (s32[16]{0:T(128)S(1)}, s32[16]{0:T(128)}, u32[]{:S(2)}) copy-start(s32[16]{0:T(128)} %param.18) | copy-start | bytes 196
  47.2 99.7 %all-gather.8.cloned.1.call-start = ((), (), s32[]{:S(2)}) async-start(), calls=%async_computation.5 | async-start | bytes 7798784 | tf_op jit(solution)/shard_map/all_gather | solution.py:374
  48.0 135.7 %reduce-scatter.2.cloned.1.call-start = ((), (), s32[]{:S(2)}) async-start(), calls=%async_computation.6 | async-start | bytes 2064384 | tf_op jit(solution)/shard_map/reduce_scatter | solution.py:377
  73.9 21.4 %copy-start.19 = (s32[64]{0:T(128)}, s32[64]{0:T(128)S(1)}, u32[]{:S(2)}) copy-start(s32[64]{0:T(128)S(1)} %slice.47) | copy-start | bytes 772
  76.5 0.6 copy-start.17
  95.2 0.7 copy-start.6
  98.6 8.3 %copy-start.10 = (f32[192,8]{1,0:T(8,128)S(1)}, f32[192,8]{1,0:T(8,128)}, u32[]{:S(2)}) copy-start(f32[192,8]{1,0:T(8,128)} %get-tuple-element.16) | copy-start | bytes 18436
  98.6 8.3 %copy-start.3 = (f32[192,8,256]{2,1,0:T(8,128)S(1)}, f32[192,8,256]{2,1,0:T(8,128)}, u32[]{:S(2)}) copy-start(f32[192,8,256]{2,1,0:T(8,128)} %get-tuple-element.17) | copy-start | bytes 4718596
  98.6 8.3 %copy-start.18 = (s32[256]{0:T(256)S(1)}, s32[256]{0:T(256)}, u32[]{:S(2)}) copy-start(s32[256]{0:T(256)} %copy-done.17) | copy-start | bytes 3076
  114.9 11.2 %copy-start.4 = (bf16[192,8,256]{2,1,0:T(8,128)(2,1)S(1)}, bf16[192,8,256]{2,1,0:T(8,128)(2,1)}, u32[]{:S(2)}) copy-start(bf16[192,8,256]{2,1,0:T(8,128)(2,1)} %get-tuple-element.4) | copy-start | bytes 2359300
  114.9 11.2 %copy-start.8 = (bf16[1,256,576]{1,2,0:T(8,128)(2,1)S(1)}, bf16[1,256,576]{1,2,0:T(8,128)(2,1)}, u32[]{:S(2)}) copy-start(bf16[1,256,576]{1,2,0:T(8,128)(2,1)} %copy.35) | copy-start | bytes 884740
  114.9 11.2 %copy-start.13 = (f32[192,8]{0,1:T(8,128)S(1)}, f32[192,8]{0,1:T(8,128)}, u32[]{:S(2)}) copy-start(f32[192,8]{0,1:T(8,128)} %copy.40) | copy-start | bytes 18436
  127.9 4.2 %copy-start.15 = (f32[64,8]{0,1:T(8,128)S(1)}, f32[64,8]{0,1:T(8,128)}, u32[]{:S(2)}) copy-start(f32[64,8]{0,1:T(8,128)} %get-tuple-element.12) | copy-start | bytes 6148
  127.9 4.2 %copy-start.20 = (s32[64]{0:T(128)S(1)}, s32[64]{0:T(128)}, u32[]{:S(2)}) copy-start(s32[64]{0:T(128)} %copy-done.19) | copy-start | bytes 772
  127.9 4.2 %copy-start.5 = (f32[64,8,256]{2,0,1:T(8,128)S(1)}, f32[64,8,256]{2,0,1:T(8,128)}, u32[]{:S(2)}) copy-start(f32[64,8,256]{2,0,1:T(8,128)} %get-tuple-element.13) | copy-start | bytes 1572868
  132.1 1.8 copy-start.21
  133.9 1.4 copy-start.7
  135.2 1.5 copy-start.23
  146.9 6.6 %copy-start.11 = (s32[32,8]{0,1:T(8,128)S(1)}, s32[32,8]{0,1:T(8,128)}, u32[]{:S(2)}) copy-start(s32[32,8]{0,1:T(8,128)} %param.27) | copy-start | bytes 3076
  146.9 7.3 %copy-start.14 = (f32[32,8]{0,1:T(8,128)S(1)}, f32[32,8]{0,1:T(8,128)}, u32[]{:S(2)}) copy-start(f32[32,8]{0,1:T(8,128)} %param.28) | copy-start | bytes 3076
  146.9 7.9 %copy-start.12 = (bf16[3584]{0:T(1024)(128)(2,1)S(1)}, bf16[3584]{0:T(1024)(128)(2,1)}, u32[]{:S(2)}) copy-start(bf16[3584]{0:T(1024)(128)(2,1)} %param.23) | copy-start | bytes 21508
Sparse Core Ops, SparseCore 0:
  9.7 32.1 all-gather.3
  47.3 31.5 all-gather.5
  81.1 65.7 all-gather.7
  153.6 29.9 reduce-scatter.1
where the time goes:
time: 267 us; the launch traced here: 265 us
  Pallas kernels  73.4 us (27%)
  waiting for transfers between devices  46.2 us (17%)
  blocking collectives  43.7 us (16%)
  matrix products  41.4 us (16%)
  local copies, waits for them, and re-layouts  23.3 us (9%)
  between operations  16 us (6%)
  other arithmetic  13.4 us (5%)
  starting transfers between devices  7.74 us (3%)
    pallas_call x1, Pallas kernels, moe(): pl.pallas_call(functools.partial(moe_kernel, (n_dp, n_ep, chunks)), out_s...  73.4 us
    reduce_scatter x1, waiting for transfers between devices, shards(): lax.psum_scatter(projected.astype(jnp.bfloat16), 'ep', scatter_dimension=...  27.5 us
    all_gather x1, blocking collectives, shards(): lax.all_gather(new_latents, 'ep', axis=1, tiled=True)  18.6 us
    all_gather x1, blocking collectives, shards(): lax.all_gather(moved_shard[prefix_part:], 'ep', axis=0, tiled=True)  12.9 us
    dot_general x2, matrix products, attend(): jnp.einsum('thj,jl->thl', exp_old.astype(jnp.bfloat16), prefix_all[:, :la...  12.5 us
    dot_general x2, matrix products, attend(): jnp.einsum('thc,jc->thj', queries, prefix_all, preferred_element_type=jnp...  12.4 us
    all_to_all x1, blocking collectives, shards(): lax.all_to_all(routed, 'dp', split_axis=0, concat_axis=0, tiled=True)  12.2 us
    unnamed x53, local copies, waits for them, and re-layouts  11.1 us
  transfers between devices with their start and end apart: 5, of which 3 were waited for; matrix products, arithmetic and copies ran while one was open for 25% of the time, Pallas kernels for 0%

commit v1 on v0

--- a/solution.py
+++ b/solution.py
@@ -1,4 +1,5 @@
 import functools
+import math
 
 import jax
 import jax.numpy as jnp
@@ -11,43 +12,8 @@
 
 
 score_scale = 192.0 ** (-0.5)
+exp2_scale = score_scale * math.log2(math.e)
 norm_eps = 1e-06
-
-
-def attend(queries, keys, length, positions, prefix_len, latent_width):
-    prefix_all = keys[:prefix_len]
-    new_all = keys[prefix_len:]
-    scores_old = (
-        jnp.einsum("thc,jc->thj", queries, prefix_all, preferred_element_type=jnp.float32)
-        * score_scale
-    )
-    scores_new = (
-        jnp.einsum("thc,jc->thj", queries, new_all, preferred_element_type=jnp.float32)
-        * score_scale
-    )
-    old_pos = lax.broadcasted_iota(jnp.int32, scores_old.shape, 2)
-    old_valid = old_pos < length
-    new_pos = lax.broadcasted_iota(jnp.int32, scores_new.shape, 2)
-    new_valid = new_pos <= positions[:, None, None]
-    scores_old = jnp.where(old_valid, scores_old, -1e30)
-    scores_new = jnp.where(new_valid, scores_new, -1e30)
-    row_max = jnp.maximum(jnp.max(scores_old, axis=2), jnp.max(scores_new, axis=2))[:, :, None]
-    exp_old = jnp.where(old_valid, jnp.exp(scores_old - row_max), 0.0)
-    exp_new = jnp.where(new_valid, jnp.exp(scores_new - row_max), 0.0)
-    weight_sum = jnp.sum(exp_old, axis=2) + jnp.sum(exp_new, axis=2)
-    weighted = jnp.einsum(
-        "thj,jl->thl",
-        exp_old.astype(jnp.bfloat16),
-        prefix_all[:, :latent_width],
-        preferred_element_type=jnp.float32,
-    )
-    weighted = weighted + jnp.einsum(
-        "thj,jl->thl",
-        exp_new.astype(jnp.bfloat16),
-        new_all[:, :latent_width],
-        preferred_element_type=jnp.float32,
-    )
-    return (weighted / weight_sum[:, :, None]).astype(jnp.bfloat16)
 
 
 MESH = pl.DeviceIdType.MESH
@@ -71,7 +37,6 @@
     res_ref,
     gain_ref,
     ids_ref,
-    ids_t_ref,
     gates_ref,
     gate_hbm,
     up_hbm,
@@ -158,28 +123,24 @@
     def mm(a, b):
         return jnp.dot(a, b, preferred_element_type=jnp.float32)
 
-    slot_col = lax.broadcasted_iota(jnp.int32, (rows, tokens), 0)
-    slot_row = lax.broadcasted_iota(jnp.int32, (tokens, rows), 1)
-    named_t = jnp.zeros((rows, tokens), jnp.float32)
-    named = jnp.zeros((tokens, rows), jnp.float32)
-    weight = jnp.zeros((tokens, rows), jnp.float32)
+    slot = lax.broadcasted_iota(jnp.int32, (rows, tokens), 0)
+    named = jnp.zeros((rows, tokens), jnp.float32)
+    weight = jnp.zeros((rows, tokens), jnp.float32)
     for k in range(TOP):
-        named_t += jnp.where(ids_t_ref[k : k + 1, :] == (slot_col >> 1), 1.0, 0.0)
-        hit = ids_ref[:, k : k + 1] == (slot_row >> 1)
+        hit = ids_ref[k : k + 1, :] == (slot >> 1)
         named += jnp.where(hit, 1.0, 0.0)
-        weight += jnp.where(hit, gates_ref[:, k : k + 1], 0.0)
+        weight += jnp.where(hit, gates_ref[k : k + 1, :], 0.0)
     first = lax.broadcasted_iota(jnp.int32, (tokens, tokens), 0)
     second = lax.broadcasted_iota(jnp.int32, (tokens, tokens), 1)
-    before_t = jnp.where(first < second, 1.0, 0.0).astype(jnp.bfloat16)
-    before = jnp.where(second < first, 1.0, 0.0).astype(jnp.bfloat16)
-    rank_t = mm(named_t.astype(jnp.bfloat16), before_t)
-    rank = mm(before, named.astype(jnp.bfloat16))
-    pick = jnp.where(rank_t == (slot_col & 1).astype(jnp.float32), named_t, 0.0).astype(
-        jnp.bfloat16
-    )
-    weight = jnp.where(rank == (slot_row & 1).astype(jnp.float32), weight, 0.0)
+    before = jnp.where(first < second, 1.0, 0.0).astype(jnp.bfloat16)
+    same = jnp.where(first == second, 1.0, 0.0).astype(jnp.bfloat16)
+    chosen = mm(named.astype(jnp.bfloat16), before) == (slot & 1).astype(jnp.float32)
+    pick = jnp.where(chosen, named, 0.0).astype(jnp.bfloat16)
+    weight = jnp.where(chosen, weight, 0.0)
     weight_high = weight.astype(jnp.bfloat16)
     weight_low = (weight - weight_high.astype(jnp.float32)).astype(jnp.bfloat16)
+    weight_high = contract_last(same, weight_high).astype(jnp.bfloat16)
+    weight_low = contract_last(same, weight_low).astype(jnp.bfloat16)
     weights = jnp.concatenate([weight_high, weight_low], axis=0)
     to = lax.broadcasted_iota(jnp.int32, (rows, rows), 0)
     frm = lax.broadcasted_iota(jnp.int32, (rows, rows), 1)
@@ -252,7 +213,7 @@
     return pl.pallas_call(
         functools.partial(moe_kernel, (n_dp, n_ep, chunks)),
         out_shape=jax.ShapeDtypeStruct((tokens, width), jnp.bfloat16),
-        in_specs=[vmem] * 6 + [hbm] * 3,
+        in_specs=[vmem] * 5 + [hbm] * 3,
         out_specs=vmem,
         scratch_shapes=[
             pltpu.VMEM((width, units), jnp.bfloat16),
@@ -281,12 +242,435 @@
         attention,
         residual,
         norm_gain.reshape(1, -1),
-        expert_ids,
         expert_ids.T,
-        gate_weights,
+        gate_weights.T,
         expert_gate,
         expert_up,
         expert_down,
+    )
+
+
+def contract_last(a, b):
+    return lax.dot_general(a, b, (((1,), (1,)), ((), ())), preferred_element_type=jnp.float32)
+
+
+def attend(q, keys, length, positions, prefix_len, lat):
+    s_old = contract_last(q, keys[0:prefix_len, :])
+    s_new = contract_last(q, keys[prefix_len:, :])
+    old_pos = lax.broadcasted_iota(jnp.int32, (1, prefix_len), 1)
+    s_old = s_old + jnp.where(old_pos < length, 0.0, -1e30)
+    new_pos = lax.broadcasted_iota(jnp.int32, s_new.shape, 1)
+    s_new = jnp.where(new_pos <= positions, s_new, -1e30)
+    top = jnp.maximum(
+        jnp.max(s_old, axis=1, keepdims=True), jnp.max(s_new, axis=1, keepdims=True)
+    )
+    e_old = jnp.exp2((s_old - top) * exp2_scale)
+    e_new = jnp.exp2((s_new - top) * exp2_scale)
+    weight_sum = jnp.sum(e_old, axis=1, keepdims=True) + jnp.sum(e_new, axis=1, keepdims=True)
+    weighted = jnp.dot(
+        e_old.astype(jnp.bfloat16), keys[0:prefix_len, 0:lat], preferred_element_type=jnp.float32
+    )
+    weighted += jnp.dot(
+        e_new.astype(jnp.bfloat16), keys[prefix_len:, 0:lat], preferred_element_type=jnp.float32
+    )
+    return (weighted * (1.0 / weight_sum)).astype(jnp.bfloat16)
+
+
+SIDE = 4
+
+
+def attention_kernel(
+    lengths_ref,
+    sources_ref,
+    owner_ref,
+    prefix_ref,
+    new_ref,
+    proj_ref,
+    queries_hbm,
+    value_up_hbm,
+    att_ref,
+    decode_ref,
+    q_raw,
+    value_up,
+    q_home,
+    q_late,
+    keys_own,
+    keys_moved,
+    spread,
+    staged,
+    news,
+    proj,
+    heads,
+    part,
+    part_b,
+    pair,
+    summed,
+    gathered,
+    z_recv,
+    y_recv,
+    dp_recv,
+    x_recv,
+    pair_recv,
+    last_recv,
+    sends,
+    load_sems,
+):
+    dp, ep = lax.axis_index("dp"), lax.axis_index("ep")
+    x, y = dp // SIDE, lax.rem(dp, SIDE)
+    z, core = ep // 2, lax.rem(ep, 2)
+    n_dp = SIDE * SIDE
+    n_ep = 2 * SIDE
+    prefix_part, new_part = prefix_ref.shape[2], new_ref.shape[1]
+    prefix_len = prefix_part * n_ep
+    shard_rows = prefix_part + new_part
+    head_count, lat, vh = value_up.shape
+    span = q_raw.shape[2]
+    late = span // 4
+    home = span - late
+    tokens = span // n_ep
+    col_part = proj_ref.shape[0]
+    cols = col_part * SIDE
+    piece = prefix_part // n_dp
+
+    def around(a, k):
+        return lax.rem(a + k + SIDE, SIDE)
+
+    def device(x2, y2, z2, core2):
+        return (x2 * SIDE + y2, z2 * 2 + core2)
+
+    right_z, left_z = device(x, y, around(z, 1), core), device(x, y, around(z, -1), core)
+    right_y, left_y = device(x, around(y, 1), z, core), device(x, around(y, -1), z, core)
+    sibling = device(x, y, z, 1 - core)
+
+    load_q = pltpu.make_async_copy(queries_hbm, q_raw, load_sems.at[0])
+    load_q.start()
+    load_v = pltpu.make_async_copy(value_up_hbm, value_up, load_sems.at[1])
+    load_v.start()
+
+    barrier = pltpu.get_barrier_semaphore()
+
+    def hello(to):
+        pl.semaphore_signal(barrier, inc=1, device_id=to, device_id_type=MESH)
+
+    partners(n_dp, dp, lambda p: hello((p, ep)))
+    for kz in range(1, SIDE):
+        for kx in range(SIDE):
+            hello(device(around(x, kx), y, around(z, kz), core))
+    hello(sibling)
+
+    def send(src, dst, to, send_sem, recv_sem):
+        pltpu.make_async_remote_copy(
+            src_ref=src,
+            dst_ref=dst,
+            send_sem=send_sem,
+            recv_sem=recv_sem,
+            device_id=to,
+            device_id_type=MESH,
+        ).start()
+
+    def wait(sem, ref):
+        pltpu.make_async_copy(ref, ref, sem).wait()
+
+    def key_parts(buf, z2, core2, half):
+        at = z2 * 2 + core2
+        n, m = (prefix_part // 2, new_part // 2) if half is not None else (prefix_part, new_part)
+        half = half or 0
+        old = pl.multiple_of(at * prefix_part + half * n, n)
+        new = pl.multiple_of(prefix_len + at * new_part + half * m, m)
+        return [buf.at[pl.ds(old, n)], buf.at[pl.ds(new, m)]]
+
+    eye_a = lax.broadcasted_iota(jnp.int32, (span, span), 0)
+    eye_b = lax.broadcasted_iota(jnp.int32, (span, span), 1)
+    eye = jnp.where(eye_a == eye_b, 1.0, 0.0).astype(jnp.bfloat16)
+    keys_own[block_rows(ep, prefix_part)] = contract_last(eye, prefix_ref[0]).astype(jnp.bfloat16)
+    keys_own[pl.ds(pl.multiple_of(prefix_len + ep * new_part, new_part), new_part)] = new_ref[0]
+    proj[block_rows(y, col_part)] = proj_ref[...]
+
+    pl.semaphore_wait(barrier, n_dp - 1 + (SIDE - 1) * SIDE + 1)
+
+    def ring_start(refs, right, left, send_sem, recv):
+        for half in (0, 1):
+            for ref in refs(0, half):
+                send(ref, ref, right, send_sem, recv.at[half])
+            for ref in refs(0, 1 - half):
+                send(ref, ref, left, send_sem, recv.at[2 + 1 - half])
+
+    def ring_forward(refs, right, left, send_sem, recv, half_ref):
+        wait(recv.at[0], half_ref)
+        for ref in refs(-1, 0):
+            send(ref, ref, right, send_sem, recv.at[4])
+        wait(recv.at[3], half_ref)
+        for ref in refs(1, 1):
+            send(ref, ref, left, send_sem, recv.at[5])
+
+    class Keys:
+        def __init__(self, i, buf):
+            self.i, self.buf = i, buf
+            self.recv = z_recv.at[i]
+            self.half = buf.at[pl.ds(0, shard_rows // 2)]
+            self.full = buf.at[pl.ds(0, shard_rows)]
+
+        def refs(self, k, half):
+            return key_parts(self.buf, around(z, k), core, half)
+
+        def start(self):
+            ring_start(self.refs, right_z, left_z, sends.at[self.i], self.recv)
+            self.share(0, 6)
+
+        def share(self, k, sem):
+            for ref in self.refs(k, None):
+                send(ref, ref, sibling, sends.at[self.i], self.recv.at[sem])
+
+        def forward(self):
+            ring_forward(self.refs, right_z, left_z, sends.at[self.i], self.recv, self.half)
+
+        def forward_near(self):
+            wait(self.recv.at[1], self.half)
+            self.share(-1, 7)
+            wait(self.recv.at[2], self.half)
+            self.share(1, 8)
+
+        def forward_far(self):
+            wait(self.recv.at[4], self.half)
+            wait(self.recv.at[5], self.half)
+            self.share(2, 9)
+
+        def finish(self):
+            for sem in range(6, 10):
+                wait(self.recv.at[sem], self.full)
+
+    own, moved = Keys(0, keys_own), Keys(1, keys_moved)
+
+    own.start()
+    prefix_at = ep * prefix_part
+
+    def spread_to(p):
+        rows = pl.multiple_of(prefix_at + p * piece, piece)
+        send(keys_own.at[pl.ds(rows, piece)], spread.at[dp], (p, ep), sends.at[2], dp_recv.at[0])
+
+    partners(n_dp, dp, spread_to)
+    spread[dp] = keys_own[pl.ds(pl.multiple_of(prefix_at + dp * piece, piece), piece)]
+    news[dp] = new_ref[0]
+    partners(
+        n_dp,
+        dp,
+        lambda p: send(news.at[dp], news.at[dp], (p, ep), sends.at[3], dp_recv.at[1]),
+    )
+
+    def proj_refs(k, half):
+        n = col_part // 2
+        start = pl.multiple_of(around(y, k) * col_part + half * n, n)
+        return [proj.at[pl.ds(start, n)]]
+
+    ring_start(proj_refs, right_y, left_y, sends.at[4], y_recv)
+
+    load_q.wait()
+
+    def turn_head(h):
+        rows = contract_last(eye, q_raw[h]).astype(jnp.bfloat16)
+        q_home[h // 2, pl.ds((h % 2) * home, home)] = rows[:home]
+        q_late[pl.ds(h * late, late)] = rows[home:]
+
+    for h in range(head_count // 2):
+        turn_head(h)
+    own.forward()
+    wait(dp_recv.at[0], keys_own.at[pl.ds(0, prefix_part - piece)])
+
+    def stage(s, carry):
+        staged[s] = spread[sources_ref[s]]
+        return carry
+
+    lax.fori_loop(0, n_dp, stage, 0)
+    landing = keys_moved.at[pl.ds(pl.multiple_of(prefix_at + dp * piece, piece), piece)]
+    partners(
+        n_dp,
+        dp,
+        lambda p: send(staged.at[p], landing, (p, ep), sends.at[5], dp_recv.at[2]),
+    )
+    keys_moved[pl.ds(pl.multiple_of(prefix_at + dp * piece, piece), piece)] = staged[dp]
+    for h in range(head_count // 2, head_count):
+        turn_head(h)
+    own.forward_near()
+    source = sources_ref[dp]
+    given = jnp.int32(0)
+    for i in range(n_dp):
+        given = jnp.maximum(given, jnp.where(owner_ref[i] == dp, i, 0))
+    wait(dp_recv.at[1], keys_own.at[pl.ds(0, (n_dp - 1) * new_part)])
+    decode_ref[0] = news[given]
+    keys_moved[pl.ds(pl.multiple_of(prefix_len + ep * new_part, new_part), new_part)] = news[source]
+    wait(dp_recv.at[2], keys_own.at[pl.ds(0, prefix_part - piece)])
+    moved.start()
+    own.forward_far()
+    ring_forward(proj_refs, right_y, left_y, sends.at[4], y_recv, proj.at[pl.ds(0, col_part // 2)])
+    own.finish()
+    load_v.wait()
+
+    def send_heads(i, rows, lanes):
+        for k in (2, 1, 3):
+            ref = heads.at[x, rows, lanes]
+            send(ref, ref, device(around(x, k), y, z, core), sends.at[6 + i], x_recv.at[i])
+
+    home_row = lax.broadcasted_iota(jnp.int32, (2 * home, 1), 0)
+    home_pos = jnp.where(home_row >= home, home_row - home, home_row)
+    pairs = head_count // 2
+    for i in range(pairs):
+        out = attend(q_home[i], keys_own, lengths_ref[dp], home_pos, prefix_len, lat)
+        for j in range(2):
+            h = 2 * i + j
+            heads[x, pl.ds(0, home), pl.ds(h * vh, vh)] = jnp.dot(
+                out[j * home : (j + 1) * home], value_up[h], preferred_element_type=jnp.float32
+            ).astype(jnp.bfloat16)
+        send_heads(i, pl.ds(0, home), pl.ds(2 * i * vh, 2 * vh))
+        if i == 0:
+            moved.forward()
+        if i == 1:
+            moved.forward_near()
+        if i == 2:
+            moved.forward_far()
+    moved.finish()
+    late_row = lax.broadcasted_iota(jnp.int32, (head_count * late, 1), 0)
+    late_pos = lax.rem(late_row, late) + home
+    out = attend(q_late[...], keys_moved, lengths_ref[source], late_pos, prefix_len, lat)
+    for h in range(head_count):
+        heads[x, pl.ds(home, late), pl.ds(h * vh, vh)] = jnp.dot(
+            out[h * late : (h + 1) * late], value_up[h], preferred_element_type=jnp.float32
+        ).astype(jnp.bfloat16)
+    send_heads(pairs, pl.ds(home, late), pl.ds(0, head_count * vh))
+
+    for i in (1, 2, 4, 5):
+        wait(y_recv.at[i], proj.at[pl.ds(0, col_part // 2)])
+
+    order = (0, 2, 1, 3)
+
+    def project(k):
+        xk = around(x, k)
+        out = contract_last(heads[xk], proj[...])
+        part[xk] = out
+        part_b[xk] = out.astype(jnp.bfloat16)
+        for kz in range(SIDE):
+            rows = block_rows(kz * 2 + 1 - core, tokens)
+            send(
+                part_b.at[xk, rows],
+                pair.at[xk, pl.ds(kz * tokens, tokens)],
+                sibling,
+                sends.at[11],
+                pair_recv.at[k],
+            )
+
+    def pass_on(k):
+        xk = around(x, k)
+        wait(pair_recv.at[k], pair.at[0])
+        for kz in (2, 1, 3, 0):
+            zk = around(z, kz)
+            mine = part[xk, block_rows(zk * 2 + core, tokens)]
+            both = mine + pair[xk, block_rows(zk, tokens)].astype(jnp.float32)
+            both = both.astype(jnp.bfloat16)
+            if k == 0 and kz == 0:
+                gathered[block_rows(x * SIDE + z, tokens)] = both
+                continue
+            at = block_rows(xk * SIDE + zk, tokens)
+            summed[at] = both
+            send(
+                summed.at[at],
+                gathered.at[block_rows(x * SIDE + z, tokens)],
+                device(xk, y, zk, core),
+                sends.at[12],
+                last_recv,
+            )
+
+    project(0)
+    wait(x_recv.at[pairs], heads.at[0, pl.ds(0, 3 * late)])
+    for i in range(pairs):
+        wait(x_recv.at[i], heads.at[0, pl.ds(0, 3 * home * 2 // head_count)])
+    project(2)
+    project(1)
+    pass_on(2)
+    project(3)
+    pass_on(1)
+    pass_on(3)
+    pass_on(0)
+    wait(last_recv, gathered.at[pl.ds(0, (n_dp - 1) * tokens)])
+    for k in range(SIDE):
+        total = gathered[pl.ds(k * SIDE * tokens, tokens)].astype(jnp.float32)
+        for j in range(1, SIDE):
+            total += gathered[pl.ds((k * SIDE + j) * tokens, tokens)].astype(jnp.float32)
+        att_ref[:, pl.ds(k * cols, cols)] = total
+
+    for i, buf in enumerate((keys_own, keys_moved)):
+        wait(sends.at[i], buf.at[pl.ds(0, 3 * shard_rows + 4 * shard_rows)])
+    wait(sends.at[2], keys_own.at[pl.ds(0, prefix_part - piece)])
+    wait(sends.at[3], keys_own.at[pl.ds(0, (n_dp - 1) * new_part)])
+    wait(sends.at[4], proj.at[pl.ds(0, 3 * col_part)])
+    wait(sends.at[5], keys_own.at[pl.ds(0, prefix_part - piece)])
+    for i in range(pairs):
+        wait(sends.at[6 + i], heads.at[0, pl.ds(0, 3 * home * 2 // head_count)])
+    wait(sends.at[6 + pairs], heads.at[0, pl.ds(0, 3 * late)])
+    wait(sends.at[11], summed)
+    wait(sends.at[12], summed.at[pl.ds(0, (n_dp - 1) * tokens)])
+
+
+def attention(queries, prefix_latents, new_latents, lengths, sources, value_up, out_proj, owner):
+    span, head_count, key_width = queries.shape
+    _, lat, vh = value_up.shape
+    n_dp, n_ep = lax.axis_size("dp"), lax.axis_size("ep")
+    late = span // 4
+    home = span - late
+    prefix_part, new_part = prefix_latents.shape[1], new_latents.shape[1]
+    key_rows = (prefix_part + new_part) * n_ep
+    rows, col_part = out_proj.shape
+    cols = col_part * SIDE
+    tokens = span // n_ep
+    vmem = pl.BlockSpec(memory_space=pltpu.VMEM)
+    smem = pl.BlockSpec(memory_space=pltpu.SMEM)
+    hbm = pl.BlockSpec(memory_space=pl.ANY)
+    bf16, f32 = jnp.bfloat16, jnp.float32
+    return pl.pallas_call(
+        attention_kernel,
+        out_shape=(
+            jax.ShapeDtypeStruct((tokens, cols * SIDE), f32),
+            jax.ShapeDtypeStruct(new_latents.shape, bf16),
+        ),
+        in_specs=[smem] * 3 + [vmem] * 3 + [hbm] * 2,
+        out_specs=(vmem, vmem),
+        scratch_shapes=[
+            pltpu.VMEM((head_count, key_width, span), bf16),
+            pltpu.VMEM(value_up.shape, bf16),
+            pltpu.VMEM((head_count // 2, 2 * home, key_width), bf16),
+            pltpu.VMEM((head_count * late, key_width), bf16),
+            pltpu.VMEM((key_rows, key_width), bf16),
+            pltpu.VMEM((key_rows, key_width), bf16),
+            pltpu.VMEM((n_dp, prefix_part // n_dp, key_width), bf16),
+            pltpu.VMEM((n_dp, prefix_part // n_dp, key_width), bf16),
+            pltpu.VMEM((n_dp, new_part, key_width), bf16),
+            pltpu.VMEM((cols, rows), bf16),
+            pltpu.VMEM((SIDE, span, rows), bf16),
+            pltpu.VMEM((SIDE, span, cols), f32),
+            pltpu.VMEM((SIDE, span, cols), bf16),
+            pltpu.VMEM((SIDE, SIDE * tokens, cols), bf16),
+            pltpu.VMEM((n_dp * tokens, cols), bf16),
+            pltpu.VMEM((n_dp * tokens, cols), bf16),
+            pltpu.SemaphoreType.DMA((2, 10)),
+            pltpu.SemaphoreType.DMA((6,)),
+            pltpu.SemaphoreType.DMA((3,)),
+            pltpu.SemaphoreType.DMA((5,)),
+            pltpu.SemaphoreType.DMA((SIDE,)),
+            pltpu.SemaphoreType.DMA,
+            pltpu.SemaphoreType.DMA((13,)),
+            pltpu.SemaphoreType.DMA((2,)),
+        ],
+        compiler_params=pltpu.CompilerParams(
+            collective_id=2, has_side_effects=True, vmem_limit_bytes=60 * 2**20
+        ),
+        name="attention",
+    )(
+        lengths,
+        sources,
+        owner,
+        prefix_latents.transpose(0, 2, 1),
+        new_latents,
+        out_proj.T,
+        queries.transpose(1, 2, 0),
+        value_up,
     )
 
 
@@ -307,78 +691,18 @@
     gate_weights,
     decode_owner,
 ):
-    latent_width = value_up.shape[1]
-    model_width = residual.shape[1]
-    dp_count = lax.axis_size("dp")
-    ep_count = lax.axis_size("ep")
-    slot = lax.axis_index("dp")
-    span_len = queries.shape[0]
-    key_width = queries.shape[2]
-    late_rows = span_len // 4
-    home_rows = span_len - late_rows
-    prefix_part = prefix_latents.shape[1]
-    prefix_len = prefix_part * ep_count
-    prefix_all, new_all = (
-        lax.all_gather(prefix_latents, "ep", axis=1, tiled=True),
-        lax.all_gather(new_latents, "ep", axis=1, tiled=True),
-    )
-    own_keys = jnp.concatenate([prefix_all[0], new_all[0]], axis=0)
-    positions = jnp.arange(span_len, dtype=jnp.int32)
-    source = span_sources[slot]
-    slot_ids = jnp.arange(dp_count, dtype=jnp.int32)
-    own_length = prefix_lengths[slot]
-    first = attend(
-        queries[:home_rows], own_keys, own_length, positions[:home_rows], prefix_len, latent_width
-    )
-    pieces = jnp.concatenate(
-        [
-            prefix_latents.reshape(dp_count, -1, key_width),
-            new_latents.reshape(dp_count, -1, key_width),
-        ],
-        axis=1,
-    )
-    old_rows = prefix_part // dp_count
-    spread = lax.all_to_all(pieces, "dp", split_axis=0, concat_axis=0, tiled=True)
-    given = jnp.zeros_like(decode_owner).at[decode_owner].set(slot_ids)
-    routed = jnp.concatenate([spread[span_sources], spread[given][:, old_rows:]], axis=1)
-    arrived = lax.all_to_all(routed, "dp", split_axis=0, concat_axis=0, tiled=True)
-    piece_rows = pieces.shape[1]
-    moved_shard = jnp.concatenate(
-        [
-            arrived[:, :old_rows].reshape(-1, key_width),
-            arrived[:, old_rows:piece_rows].reshape(-1, key_width),
-        ],
-        axis=0,
-    )
-    decode_latents = arrived[:, piece_rows:].reshape(new_latents.shape)
-    moved_prefix, moved_new = (
-        lax.all_gather(moved_shard[:prefix_part], "ep", axis=0, tiled=True),
-        lax.all_gather(moved_shard[prefix_part:], "ep", axis=0, tiled=True),
-    )
-    moved_keys = jnp.concatenate([moved_prefix, moved_new], axis=0)
-    last = attend(
-        queries[home_rows:],
-        moved_keys,
-        prefix_lengths[source],
-        positions[home_rows:],
-        prefix_len,
-        latent_width,
-    )
-    latent_out = jnp.concatenate([first, last], axis=0)
-    head_rows = jnp.einsum(
-        "thl,hlv->thv", latent_out, value_up, preferred_element_type=jnp.float32
-    ).astype(jnp.bfloat16)
-    head_rows = head_rows.reshape(span_len, -1)
-    projected = jnp.dot(
-        head_rows,
-        lax.all_gather(out_proj, "dp", axis=1, tiled=True),
-        preferred_element_type=jnp.float32,
-    )
-    attention = lax.psum_scatter(
-        projected.astype(jnp.bfloat16), "ep", scatter_dimension=0, tiled=True
+    attention_sum, decode_latents = attention(
+        queries,
+        prefix_latents,
+        new_latents,
+        prefix_lengths,
+        span_sources,
+        value_up,
+        out_proj,
+        decode_owner,
     )
     layer_out = moe(
-        attention,
+        attention_sum,
         residual,
         norm_gain,
         expert_ids,

time: 267 us -> 160 us (0.60)
  Pallas kernels: 73.4 us -> 156 us
  waiting for transfers between devices: 46.2 us -> 0 us
  blocking collectives: 43.7 us -> 0 us
  matrix products: 41.4 us -> 0 us
  local copies, waits for them, and re-layouts: 23.3 us -> 3.57 us
  between operations: 16 us -> 0.66 us
  other arithmetic: 13.4 us -> 0 us
  starting transfers between devices: 7.74 us -> 0 us
    pallas_call x0 -> x1, Pallas kernels: none -> 85.8 us  [attention(): pl.pallas_call(attention_kernel, out_shape=(jax.ShapeDtypeStruct((tokens,...]
    dot_general x10 -> x0, matrix products: 41.4 us -> none  [the longest x2 12.5 us: attend(): jnp.einsum('thj,jl->thl', exp_old.astype(jnp.bfloat16), prefix_all[:, :la...]
    all_gather x2 -> x0, blocking collectives: 31.5 us -> none  [the longest x1 18.6 us: shards(): lax.all_gather(new_latents, 'ep', axis=1, tiled=True)]
    reduce_scatter x1 -> x0, waiting for transfers between devices: 27.5 us -> none  [shards(): lax.psum_scatter(projected.astype(jnp.bfloat16), 'ep', scatter_dimension=...]
    all_to_all x1 -> x0, blocking collectives: 12.2 us -> none  [shards(): lax.all_to_all(routed, 'dp', split_axis=0, concat_axis=0, tiled=True)]
    all_gather x3 -> x0, waiting for transfers between devices: 9.39 us -> none  [the longest x1 9.39 us: shards(): lax.all_gather(out_proj, 'dp', axis=1, tiled=True)]
    unnamed x53 -> x4, local copies, waits for them, and re-layouts: 11.1 us -> 2.26 us
    all_to_all x1 -> x0, waiting for transfers between devices: 7.92 us -> none  [shards(): lax.all_to_all(pieces, 'dp', split_axis=0, concat_axis=0, tiled=True)]
  transfers between devices with their start and end apart: 5 -> 0, of which waited for: 3 -> 0; matrix products, arithmetic and copies ran while one was open for 25% -> 0% of each run, Pallas kernels for 0% -> 0%
where the time goes in v1:
time: 160 us
  Pallas kernels  156 us (98%)
  local copies, waits for them, and re-layouts  3.57 us (2%)
    pallas_call x1, Pallas kernels, attention(): pl.pallas_call(attention_kernel, out_shape=(jax.ShapeDtypeStruct((tokens,...  85.8 us
    pallas_call x1, Pallas kernels, moe(): pl.pallas_call(functools.partial(moe_kernel, (n_dp, n_ep, chunks)), out_s...  69.8 us

profile of v1, /device:TPU:1, one launch (start us, length us, event | category | flops | bytes accessed | tf_op | source)
XLA Modules:
  0.0 159.8 jit_solution(871521166219785698)
XLA Ops:
  0.6 1.3 reshape.7.gain_ref
  1.9 85.8 %attention.1 = (f32[32,3584]{1,0:T(8,128)}, bf16[1,32,576]{2,1,0:T(8,128)(2,1)}) custom-call(s32[16]{0:T(128)} %lengths_ref.1, s32[16]{0:T(128)} %sources_ref.1, s32[16]{0:T(128)} %owner_ref.1, bf16[1,576,256]{2,1,0:T(8,128)(2,1)} %bitcast.7, bf16[1,32,576]{2,1,0:T(8,128)(2,1)} %new_ref.1, bf16[224,1024]{1,0:T(8,128)(2,1)} %bitcast.6, ...), custom_call_target="tpu_custom_call" | custom-call | tf_op jit(solution)/shard_map/attention/pallas_call | solution.py:627
  87.7 0.0 copy-start
  87.8 69.8 %experts.1 = bf16[32,3584]{1,0:T(8,128)(2,1)} custom-call(f32[32,3584]{1,0:T(8,128)} %get-tuple-element.4.att_ref, bf16[32,3584]{1,0:T(8,128)(2,1)} %res_ref.1, bf16[1,3584]{1,0:T(2,128)(2,1)} %reshape.7.gain_ref, s32[8,32]{1,0:T(8,128)} %bitcast.8, f32[8,32]{1,0:T(8,128)} %bitcast.9, bf16[1,3584,1024]{2,1,0:T(8,128)(2,1)} %gate_hbm.1, ...), custom_call_target="tpu_custom_call" | custom-call | tf_op jit(solution)/shard_map/experts/pallas_call | solution.py:213
  157.5 1.6 %copy.19 = bf16[32,3584]{1,0:T(8,128)(2,1)} copy(bf16[32,3584]{1,0:T(8,128)(2,1)} %experts.1) | data formatting | bytes 458752
  159.2 0.0 copy-done
  159.2 0.6 copy.20
Async XLA Ops:
  87.7 71.4 %copy-start = (bf16[1,32,576]{2,1,0:T(8,128)(2,1)S(1)}, bf16[1,32,576]{2,1,0:T(8,128)(2,1)}, u32[]{:S(2)}) copy-start(bf16[1,32,576]{2,1,0:T(8,128)(2,1)} %get-tuple-element.9) | copy-start | bytes 110596

commit v2 on v1

--- a/solution.py
+++ b/solution.py
@@ -101,6 +101,7 @@
         partners(n_dp, dp, each)
         dst[c, block_rows(dp, dp_block)] = src[c, block_rows(dp, dp_block)]
 
+
     def send_ep(stage, c, src, dst):
         def each(p):
             pltpu.make_async_remote_copy(
@@ -115,8 +116,14 @@
         partners(n_ep, ep, each)
         dst[c, block_rows(ep, ep_block)] = src[c, block_rows(ep, ep_block)]
 
+    def over_dp(stage, c):
+        return (c % 2 == 0) == (stage in (0, 3))
+
+    def hop(stage, c, src, dst):
+        (send_dp if over_dp(stage, c) else send_ep)(stage, c, src, dst)
+
     def wait_all(sems, stage, c, ref):
-        size = rows - (dp_block if stage in (0, 3) else ep_block)
+        size = rows - (dp_block if over_dp(stage, c) else ep_block)
         part = ref.at[c, pl.ds(0, size)]
         pltpu.make_async_copy(part, part, sems.at[stage, c]).wait()
 
@@ -148,6 +155,9 @@
     by_dp = lax.rem(to >> 1, n_ep) * ep_block + (to // dp_block) * 2 + (to & 1)
     perm_ep = jnp.where(frm == by_ep, 1.0, 0.0).astype(jnp.bfloat16)
     perm_dp = jnp.where(frm == by_dp, 1.0, 0.0).astype(jnp.bfloat16)
+    picks = (pick, mm(perm_ep, pick).astype(jnp.bfloat16))
+    weights = (weights, contract_last(weights, perm_ep).astype(jnp.bfloat16))
+    perms = (perm_ep, perm_dp)
 
     hidden = res_ref[...].astype(jnp.float32) + att_ref[...].astype(jnp.float32)
     hid[...] = hidden
@@ -161,18 +171,20 @@
         normed = (hid[:, span] * scale * gain_ref[:, span].astype(jnp.float32)).astype(
             jnp.bfloat16
         )
-        s1[c] = mm(pick, normed).astype(jnp.bfloat16)
-        send_dp(0, c, s1, r1)
+        s1[c] = mm(picks[c % 2], normed).astype(jnp.bfloat16)
+        hop(0, c, s1, r1)
     for c in range(chunks):
         wait_all(recv_sems, 0, c, r1)
-        s2[c] = mm(perm_ep, r1[c]).astype(jnp.bfloat16)
-        send_ep(1, c, s2, r2)
+        s2[c] = mm(perms[c % 2], r1[c]).astype(jnp.bfloat16)
+        hop(1, c, s2, r2)
     loads[0].wait()
     loads[1].wait()
     for c in range(chunks):
         wait_all(recv_sems, 1, c, r2)
         span = pl.ds(c * cols, cols)
         x = r2[c]
+        if c % 2:
+            x = mm(perm_ep, x).astype(jnp.bfloat16)
         gate_part = mm(x, w_gate[span, :])
         up_part = mm(x, w_up[span, :])
         if c:
@@ -182,19 +194,20 @@
             total[:, pl.ds(0, hidden_units)] = gate_part
             total[:, pl.ds(hidden_units, hidden_units)] = up_part
         else:
-            act[...] = (gate_part / (1.0 + jnp.exp(-gate_part)) * up_part).astype(jnp.bfloat16)
+            act[0] = (gate_part / (1.0 + jnp.exp(-gate_part)) * up_part).astype(jnp.bfloat16)
+    act[1] = mm(perm_dp, act[0]).astype(jnp.bfloat16)
     loads[2].wait()
     for c in range(chunks):
-        o1[c] = mm(act[...], w_down[:, pl.ds(c * cols, cols)]).astype(jnp.bfloat16)
-        send_ep(2, c, o1, q1)
+        o1[c] = mm(act[c % 2], w_down[:, pl.ds(c * cols, cols)]).astype(jnp.bfloat16)
+        hop(2, c, o1, q1)
     for c in range(chunks):
         wait_all(recv_sems, 2, c, q1)
-        q2[c] = mm(perm_dp, q1[c]).astype(jnp.bfloat16)
-        send_dp(3, c, q2, q3)
+        q2[c] = mm(perms[1 - c % 2], q1[c]).astype(jnp.bfloat16)
+        hop(3, c, q2, q3)
     for c in range(chunks):
         wait_all(recv_sems, 3, c, q3)
         span = pl.ds(c * cols, cols)
-        both = mm(weights, q3[c])
+        both = mm(weights[c % 2], q3[c])
         out_ref[:, span] = (hid[:, span] + (both[:tokens] + both[tokens:])).astype(out_ref.dtype)
     for stage, ref in enumerate((s1, s2, o1, q2)):
         for c in range(chunks):
@@ -225,7 +238,7 @@
             buf,
             buf,
             pltpu.VMEM((rows, 2 * units), jnp.float32),
-            pltpu.VMEM((rows, units), jnp.bfloat16),
+            pltpu.VMEM((2, rows, units), jnp.bfloat16),
             buf,
             buf,
             buf,
@@ -295,12 +308,19 @@
     q_home,
     q_late,
     keys_own,
-    keys_moved,
-    spread,
-    staged,
-    news,
+    late_own,
+    late_in,
+    late_on,
+    rows_own,
+    rows_in,
+    rows_on,
+    rows_back,
+    news_y,
+    news_out,
+    news_x,
     proj,
     heads,
+    heads_late,
     part,
     part_b,
     pair,
@@ -328,9 +348,12 @@
     late = span // 4
     home = span - late
     tokens = span // n_ep
+    strip = tokens // 2
+    block = home // 2
+    quad = head_count // 2
     col_part = proj_ref.shape[0]
     cols = col_part * SIDE
-    piece = prefix_part // n_dp
+    piece = head_count * late // n_dp
 
     def around(a, k):
         return lax.rem(a + k + SIDE, SIDE)
@@ -403,192 +426,222 @@
         for ref in refs(1, 1):
             send(ref, ref, left, send_sem, recv.at[5])
 
-    class Keys:
-        def __init__(self, i, buf):
-            self.i, self.buf = i, buf
-            self.recv = z_recv.at[i]
-            self.half = buf.at[pl.ds(0, shard_rows // 2)]
-            self.full = buf.at[pl.ds(0, shard_rows)]
-
-        def refs(self, k, half):
-            return key_parts(self.buf, around(z, k), core, half)
-
-        def start(self):
-            ring_start(self.refs, right_z, left_z, sends.at[self.i], self.recv)
-            self.share(0, 6)
-
-        def share(self, k, sem):
-            for ref in self.refs(k, None):
-                send(ref, ref, sibling, sends.at[self.i], self.recv.at[sem])
-
-        def forward(self):
-            ring_forward(self.refs, right_z, left_z, sends.at[self.i], self.recv, self.half)
-
-        def forward_near(self):
-            wait(self.recv.at[1], self.half)
-            self.share(-1, 7)
-            wait(self.recv.at[2], self.half)
-            self.share(1, 8)
-
-        def forward_far(self):
-            wait(self.recv.at[4], self.half)
-            wait(self.recv.at[5], self.half)
-            self.share(2, 9)
-
-        def finish(self):
-            for sem in range(6, 10):
-                wait(self.recv.at[sem], self.full)
-
-    own, moved = Keys(0, keys_own), Keys(1, keys_moved)
-
-    own.start()
-    prefix_at = ep * prefix_part
-
-    def spread_to(p):
-        rows = pl.multiple_of(prefix_at + p * piece, piece)
-        send(keys_own.at[pl.ds(rows, piece)], spread.at[dp], (p, ep), sends.at[2], dp_recv.at[0])
-
-    partners(n_dp, dp, spread_to)
-    spread[dp] = keys_own[pl.ds(pl.multiple_of(prefix_at + dp * piece, piece), piece)]
-    news[dp] = new_ref[0]
-    partners(
-        n_dp,
-        dp,
-        lambda p: send(news.at[dp], news.at[dp], (p, ep), sends.at[3], dp_recv.at[1]),
-    )
+    key_half = keys_own.at[pl.ds(0, shard_rows // 2)]
+    key_full = keys_own.at[pl.ds(0, shard_rows)]
+
+    def key_refs(k, half):
+        return key_parts(keys_own, around(z, k), core, half)
+
+    def share(k, sem):
+        for ref in key_refs(k, None):
+            send(ref, ref, sibling, sends.at[0], z_recv.at[sem])
+
+    def everywhere(src, dst, send_sem, recv_sem):
+        partners(n_dp, dp, lambda p: send(src(p), dst, (p, ep), send_sem, recv_sem))
+
+    ring_start(key_refs, right_z, left_z, sends.at[0], z_recv)
+    share(0, 6)
+
+    def over_axis(along_x, src, dst, send_sem, recv_sem):
+        for k in (2, 1, 3):
+            to = device(around(x, k), y, z, core) if along_x else device(x, around(y, k), z, core)
+            send(src(k), dst, to, send_sem, recv_sem)
 
     def proj_refs(k, half):
         n = col_part // 2
         start = pl.multiple_of(around(y, k) * col_part + half * n, n)
         return [proj.at[pl.ds(start, n)]]
 
+    load_q.wait()
+    for h in range(head_count):
+        rows = contract_last(eye, q_raw[h]).astype(jnp.bfloat16)
+        late_own[pl.ds(h * late, late)] = rows[home:]
+        for b in range(2):
+            for e in range(home // tokens):
+                at = (h % quad) * block + (e % 2) * block // 2 + (e // 2) * strip
+                row = e * tokens + b * strip
+                q_home[2 * b + h // quad, pl.ds(at, strip)] = rows[row : row + strip]
+    all_late = keys_own.at[pl.ds(0, (n_dp - 1) * piece)]
+    all_rows = rows_own.at[pl.ds(0, (n_dp - 1) * piece)]
+    everywhere(
+        lambda p: late_own.at[block_rows(p, piece)], late_in.at[dp], sends.at[1], dp_recv.at[0]
+    )
+    late_in[dp] = late_own[block_rows(dp, piece)]
+    all_news = keys_own.at[pl.ds(0, (SIDE - 1) * new_part)]
+    news_y[y] = new_ref[0]
+    over_axis(False, lambda k: news_y.at[y], news_y.at[y], sends.at[3], dp_recv.at[1])
+    ring_forward(key_refs, right_z, left_z, sends.at[0], z_recv, key_half)
+    wait(z_recv.at[1], key_half)
+    share(-1, 7)
+    wait(z_recv.at[2], key_half)
+    share(1, 8)
+    wait(dp_recv.at[0], all_late)
+
+    def stage_late(i, carry):
+        slot = jnp.int32(0)
+        for s in range(n_dp):
+            slot = jnp.maximum(slot, jnp.where(sources_ref[s] == i, s, 0))
+        late_on[i] = late_in[slot]
+        return carry
+
+    lax.fori_loop(0, n_dp, stage_late, 0)
+    everywhere(
+        lambda p: late_on.at[p], q_late.at[block_rows(dp, piece)], sends.at[2], dp_recv.at[2]
+    )
+    q_late[block_rows(dp, piece)] = late_on[dp]
     ring_start(proj_refs, right_y, left_y, sends.at[4], y_recv)
-
-    load_q.wait()
-
-    def turn_head(h):
-        rows = contract_last(eye, q_raw[h]).astype(jnp.bfloat16)
-        q_home[h // 2, pl.ds((h % 2) * home, home)] = rows[:home]
-        q_late[pl.ds(h * late, late)] = rows[home:]
-
-    for h in range(head_count // 2):
-        turn_head(h)
-    own.forward()
-    wait(dp_recv.at[0], keys_own.at[pl.ds(0, prefix_part - piece)])
-
-    def stage(s, carry):
-        staged[s] = spread[sources_ref[s]]
-        return carry
-
-    lax.fori_loop(0, n_dp, stage, 0)
-    landing = keys_moved.at[pl.ds(pl.multiple_of(prefix_at + dp * piece, piece), piece)]
-    partners(
-        n_dp,
-        dp,
-        lambda p: send(staged.at[p], landing, (p, ep), sends.at[5], dp_recv.at[2]),
-    )
-    keys_moved[pl.ds(pl.multiple_of(prefix_at + dp * piece, piece), piece)] = staged[dp]
-    for h in range(head_count // 2, head_count):
-        turn_head(h)
-    own.forward_near()
-    source = sources_ref[dp]
-    given = jnp.int32(0)
-    for i in range(n_dp):
-        given = jnp.maximum(given, jnp.where(owner_ref[i] == dp, i, 0))
-    wait(dp_recv.at[1], keys_own.at[pl.ds(0, (n_dp - 1) * new_part)])
-    decode_ref[0] = news[given]
-    keys_moved[pl.ds(pl.multiple_of(prefix_len + ep * new_part, new_part), new_part)] = news[source]
-    wait(dp_recv.at[2], keys_own.at[pl.ds(0, prefix_part - piece)])
-    moved.start()
-    own.forward_far()
-    ring_forward(proj_refs, right_y, left_y, sends.at[4], y_recv, proj.at[pl.ds(0, col_part // 2)])
-    own.finish()
+    wait(z_recv.at[4], key_half)
+    wait(z_recv.at[5], key_half)
+    share(2, 9)
     load_v.wait()
-
-    def send_heads(i, rows, lanes):
-        for k in (2, 1, 3):
-            ref = heads.at[x, rows, lanes]
-            send(ref, ref, device(around(x, k), y, z, core), sends.at[6 + i], x_recv.at[i])
-
-    home_row = lax.broadcasted_iota(jnp.int32, (2 * home, 1), 0)
-    home_pos = jnp.where(home_row >= home, home_row - home, home_row)
-    pairs = head_count // 2
-    for i in range(pairs):
-        out = attend(q_home[i], keys_own, lengths_ref[dp], home_pos, prefix_len, lat)
-        for j in range(2):
-            h = 2 * i + j
-            heads[x, pl.ds(0, home), pl.ds(h * vh, vh)] = jnp.dot(
-                out[j * home : (j + 1) * home], value_up[h], preferred_element_type=jnp.float32
+    for sem in range(6, 10):
+        wait(z_recv.at[sem], key_full)
+
+    def given_to(slot):
+        given = jnp.int32(0)
+        for i in range(n_dp):
+            given = jnp.maximum(given, jnp.where(owner_ref[i] == slot, i, 0))
+        return given
+
+    def send_heads(i, refs):
+        for ref in refs:
+            over_axis(True, lambda k: ref, ref, sends.at[6 + i], x_recv.at[i])
+
+    row = lax.broadcasted_iota(jnp.int32, (quad * block, 1), 0)
+    within = row
+    for j in range(1, quad):
+        within -= jnp.where(row >= j * block, block, 0)
+    on_core = jnp.where(within >= block // 2, 1, 0)
+    within -= on_core * (block // 2)
+    home_pos = ((within // strip) * 2 + on_core) * tokens + lax.rem(within, strip)
+    half_rows = SIDE * block // 2
+
+    def home_part(b, half):
+        positions = home_pos + b * strip
+        out = attend(q_home[2 * b + half], keys_own, lengths_ref[dp], positions, prefix_len, lat)
+        for j in range(quad):
+            h = half * quad + j
+            rows = jnp.dot(
+                out[j * block : (j + 1) * block], value_up[h], preferred_element_type=jnp.float32
             ).astype(jnp.bfloat16)
-        send_heads(i, pl.ds(0, home), pl.ds(2 * i * vh, 2 * vh))
-        if i == 0:
-            moved.forward()
-        if i == 1:
-            moved.forward_near()
-        if i == 2:
-            moved.forward_far()
-    moved.finish()
+            for c in range(2):
+                at = pl.multiple_of(c * half_rows + x * (block // 2), block // 2)
+                heads[b, pl.ds(at, block // 2), pl.ds(h * vh, vh)] = rows[
+                    c * block // 2 : (c + 1) * block // 2
+                ]
+        refs = []
+        for c in range(2):
+            at = pl.multiple_of(c * half_rows + x * (block // 2), block // 2)
+            refs.append(
+                heads.at[b, pl.ds(at, block // 2), pl.ds(half * quad * vh, quad * vh)]
+            )
+        send_heads(2 * b + half, refs)
+
+    def wait_heads(i):
+        wait(x_recv.at[i], heads.at[0, pl.ds(0, (SIDE - 1) * block // 2)])
+
+    def project(i, rows):
+        n = rows.shape[0]
+        out = contract_last(rows, proj[...])
+        part[i, pl.ds(0, n)] = out
+        part_b[i, pl.ds(0, n)] = out.astype(jnp.bfloat16)
+        other = part_b.at[i, pl.ds(pl.multiple_of((1 - core) * (n // 2), n // 2), n // 2)]
+        send(other, pair.at[i, pl.ds(0, n // 2)], sibling, sends.at[11 + i], pair_recv.at[i])
+
+    def pass_on(i, n, to_z, size, offset):
+        wait(pair_recv.at[i], pair.at[i, pl.ds(0, n // 2)])
+        mine = part[i, pl.ds(pl.multiple_of(core * (n // 2), n // 2), n // 2)]
+        both = mine + pair[i, pl.ds(0, n // 2)].astype(jnp.float32)
+        summed[i, pl.ds(0, n // 2)] = both.astype(jnp.bfloat16)
+        start = (x * SIDE + z) * tokens + offset
+        landing = pl.ds(pl.multiple_of(start, size), size)
+        for k in (2, 1, 3, 0):
+            xk = around(x, k)
+            for j, zk in enumerate(to_z):
+                at = pl.multiple_of((xk * len(to_z) + j) * size, size)
+
+                def go():
+                    send(
+                        summed.at[i, pl.ds(at, size)],
+                        gathered.at[landing],
+                        device(xk, y, zk, core),
+                        sends.at[14],
+                        last_recv,
+                    )
+
+                if k:
+                    go()
+                else:
+                    pl.when(z != zk)(go)
+
+                    @pl.when(z == zk)
+                    def _():
+                        gathered[landing] = summed[i, pl.ds(at, size)]
+
+    home_part(0, 0)
+    wait(dp_recv.at[1], all_news)
+    for k in range(SIDE):
+        slot = around(x, k) * SIDE + y
+        news_out[k] = news_y[lax.rem(given_to(slot), SIDE)]
+    over_axis(True, lambda k: news_out.at[k], news_x.at[x], sends.at[15], dp_recv.at[5])
+    news_x[x] = news_out[0]
+    home_part(0, 1)
+    proj_half = proj.at[pl.ds(0, col_part // 2)]
+    ring_forward(proj_refs, right_y, left_y, sends.at[4], y_recv, proj_half)
+    wait(dp_recv.at[2], all_late)
     late_row = lax.broadcasted_iota(jnp.int32, (head_count * late, 1), 0)
     late_pos = lax.rem(late_row, late) + home
-    out = attend(q_late[...], keys_moved, lengths_ref[source], late_pos, prefix_len, lat)
+    out = attend(q_late[...], keys_own, lengths_ref[dp], late_pos, prefix_len, lat)
     for h in range(head_count):
-        heads[x, pl.ds(home, late), pl.ds(h * vh, vh)] = jnp.dot(
+        rows_own[pl.ds(h * late, late)] = jnp.dot(
             out[h * late : (h + 1) * late], value_up[h], preferred_element_type=jnp.float32
         ).astype(jnp.bfloat16)
-    send_heads(pairs, pl.ds(home, late), pl.ds(0, head_count * vh))
-
+    everywhere(
+        lambda p: rows_own.at[block_rows(p, piece)], rows_in.at[dp], sends.at[5], dp_recv.at[3]
+    )
+    rows_in[dp] = rows_own[block_rows(dp, piece)]
+    home_part(1, 0)
+    wait(dp_recv.at[3], all_rows)
+
+    def stage_rows(s, carry):
+        rows_on[s] = rows_in[sources_ref[s]]
+        return carry
+
+    lax.fori_loop(0, n_dp, stage_rows, 0)
+    everywhere(
+        lambda p: rows_on.at[p], rows_back.at[block_rows(dp, piece)], sends.at[16], dp_recv.at[4]
+    )
+    rows_back[block_rows(dp, piece)] = rows_on[dp]
     for i in (1, 2, 4, 5):
-        wait(y_recv.at[i], proj.at[pl.ds(0, col_part // 2)])
-
-    order = (0, 2, 1, 3)
-
-    def project(k):
-        xk = around(x, k)
-        out = contract_last(heads[xk], proj[...])
-        part[xk] = out
-        part_b[xk] = out.astype(jnp.bfloat16)
-        for kz in range(SIDE):
-            rows = block_rows(kz * 2 + 1 - core, tokens)
-            send(
-                part_b.at[xk, rows],
-                pair.at[xk, pl.ds(kz * tokens, tokens)],
-                sibling,
-                sends.at[11],
-                pair_recv.at[k],
-            )
-
-    def pass_on(k):
-        xk = around(x, k)
-        wait(pair_recv.at[k], pair.at[0])
-        for kz in (2, 1, 3, 0):
-            zk = around(z, kz)
-            mine = part[xk, block_rows(zk * 2 + core, tokens)]
-            both = mine + pair[xk, block_rows(zk, tokens)].astype(jnp.float32)
-            both = both.astype(jnp.bfloat16)
-            if k == 0 and kz == 0:
-                gathered[block_rows(x * SIDE + z, tokens)] = both
-                continue
-            at = block_rows(xk * SIDE + zk, tokens)
-            summed[at] = both
-            send(
-                summed.at[at],
-                gathered.at[block_rows(x * SIDE + z, tokens)],
-                device(xk, y, zk, core),
-                sends.at[12],
-                last_recv,
-            )
-
-    project(0)
-    wait(x_recv.at[pairs], heads.at[0, pl.ds(0, 3 * late)])
-    for i in range(pairs):
-        wait(x_recv.at[i], heads.at[0, pl.ds(0, 3 * home * 2 // head_count)])
-    project(2)
-    project(1)
-    pass_on(2)
-    project(3)
-    pass_on(1)
-    pass_on(3)
-    pass_on(0)
+        wait(y_recv.at[i], proj_half)
+    wait_heads(0)
+    wait_heads(1)
+    project(0, heads[0])
+    home_part(1, 1)
+    wait(dp_recv.at[4], all_rows)
+    late_part = late // 2
+    refs = []
+    for c in range(2):
+        at = pl.multiple_of(c * SIDE * late_part + x * late_part, late_part)
+        refs.append(heads_late.at[pl.ds(at, late_part)])
+        for h in range(head_count):
+            heads_late[pl.ds(at, late_part), pl.ds(h * vh, vh)] = rows_back[
+                pl.ds(h * late + c * late_part, late_part)
+            ]
+    send_heads(4, refs)
+    home_z = tuple(range(home // tokens // 2))
+    late_z = (SIDE - 1,)
+    home_rows, late_rows = SIDE * block, SIDE * late
+    pass_on(0, home_rows, home_z, strip, 0)
+    wait_heads(2)
+    wait_heads(3)
+    project(1, heads[1])
+    wait(x_recv.at[4], heads_late.at[pl.ds(0, (SIDE - 1) * late)])
+    project(2, heads_late[...])
+    pass_on(1, home_rows, home_z, strip, strip)
+    pass_on(2, late_rows, late_z, tokens, 0)
+    wait(dp_recv.at[5], all_news)
+    decode_ref[0] = news_x[given_to(dp) // SIDE]
     wait(last_recv, gathered.at[pl.ds(0, (n_dp - 1) * tokens)])
     for k in range(SIDE):
         total = gathered[pl.ds(k * SIDE * tokens, tokens)].astype(jnp.float32)
@@ -596,17 +649,21 @@
             total += gathered[pl.ds((k * SIDE + j) * tokens, tokens)].astype(jnp.float32)
         att_ref[:, pl.ds(k * cols, cols)] = total
 
-    for i, buf in enumerate((keys_own, keys_moved)):
-        wait(sends.at[i], buf.at[pl.ds(0, 3 * shard_rows + 4 * shard_rows)])
-    wait(sends.at[2], keys_own.at[pl.ds(0, prefix_part - piece)])
-    wait(sends.at[3], keys_own.at[pl.ds(0, (n_dp - 1) * new_part)])
+    wait(sends.at[0], keys_own.at[pl.ds(0, 3 * shard_rows + 4 * shard_rows)])
+    wait(sends.at[1], all_late)
+    wait(sends.at[2], all_late)
+    wait(sends.at[3], all_news)
+    wait(sends.at[15], all_news)
     wait(sends.at[4], proj.at[pl.ds(0, 3 * col_part)])
-    wait(sends.at[5], keys_own.at[pl.ds(0, prefix_part - piece)])
-    for i in range(pairs):
-        wait(sends.at[6 + i], heads.at[0, pl.ds(0, 3 * home * 2 // head_count)])
-    wait(sends.at[6 + pairs], heads.at[0, pl.ds(0, 3 * late)])
-    wait(sends.at[11], summed)
-    wait(sends.at[12], summed.at[pl.ds(0, (n_dp - 1) * tokens)])
+    wait(sends.at[5], all_rows)
+    wait(sends.at[16], all_rows)
+    for i in range(4):
+        wait(sends.at[6 + i], heads.at[0, pl.ds(0, (SIDE - 1) * block // 2)])
+    wait(sends.at[10], heads_late.at[pl.ds(0, (SIDE - 1) * late)])
+    for i in range(2):
+        wait(sends.at[11 + i], pair.at[i])
+    wait(sends.at[13], pair.at[2, pl.ds(0, late_rows // 2)])
+    wait(sends.at[14], gathered.at[pl.ds(0, (n_dp - 1) * tokens)])
 
 
 def attention(queries, prefix_latents, new_latents, lengths, sources, value_up, out_proj, owner):
@@ -615,6 +672,7 @@
     n_dp, n_ep = lax.axis_size("dp"), lax.axis_size("ep")
     late = span // 4
     home = span - late
+    late_rows = head_count * late
     prefix_part, new_part = prefix_latents.shape[1], new_latents.shape[1]
     key_rows = (prefix_part + new_part) * n_ep
     rows, col_part = out_proj.shape
@@ -635,27 +693,34 @@
         scratch_shapes=[
             pltpu.VMEM((head_count, key_width, span), bf16),
             pltpu.VMEM(value_up.shape, bf16),
-            pltpu.VMEM((head_count // 2, 2 * home, key_width), bf16),
-            pltpu.VMEM((head_count * late, key_width), bf16),
+            pltpu.VMEM((4, head_count // 2 * (home // 2), key_width), bf16),
+            pltpu.VMEM((late_rows, key_width), bf16),
             pltpu.VMEM((key_rows, key_width), bf16),
-            pltpu.VMEM((key_rows, key_width), bf16),
-            pltpu.VMEM((n_dp, prefix_part // n_dp, key_width), bf16),
-            pltpu.VMEM((n_dp, prefix_part // n_dp, key_width), bf16),
-            pltpu.VMEM((n_dp, new_part, key_width), bf16),
+            pltpu.VMEM((late_rows, key_width), bf16),
+            pltpu.VMEM((n_dp, late_rows // n_dp, key_width), bf16),
+            pltpu.VMEM((n_dp, late_rows // n_dp, key_width), bf16),
+            pltpu.VMEM((late_rows, vh), bf16),
+            pltpu.VMEM((n_dp, late_rows // n_dp, vh), bf16),
+            pltpu.VMEM((n_dp, late_rows // n_dp, vh), bf16),
+            pltpu.VMEM((late_rows, vh), bf16),
+            pltpu.VMEM((SIDE, new_part, key_width), bf16),
+            pltpu.VMEM((SIDE, new_part, key_width), bf16),
+            pltpu.VMEM((SIDE, new_part, key_width), bf16),
             pltpu.VMEM((cols, rows), bf16),
-            pltpu.VMEM((SIDE, span, rows), bf16),
-            pltpu.VMEM((SIDE, span, cols), f32),
-            pltpu.VMEM((SIDE, span, cols), bf16),
-            pltpu.VMEM((SIDE, SIDE * tokens, cols), bf16),
+            pltpu.VMEM((2, SIDE * home // 2, rows), bf16),
+            pltpu.VMEM((SIDE * late, rows), bf16),
+            pltpu.VMEM((3, SIDE * home // 2, cols), f32),
+            pltpu.VMEM((3, SIDE * home // 2, cols), bf16),
+            pltpu.VMEM((3, SIDE * home // 4, cols), bf16),
+            pltpu.VMEM((3, SIDE * home // 4, cols), bf16),
             pltpu.VMEM((n_dp * tokens, cols), bf16),
-            pltpu.VMEM((n_dp * tokens, cols), bf16),
-            pltpu.SemaphoreType.DMA((2, 10)),
+            pltpu.SemaphoreType.DMA((10,)),
             pltpu.SemaphoreType.DMA((6,)),
+            pltpu.SemaphoreType.DMA((6,)),
+            pltpu.SemaphoreType.DMA((5,)),
             pltpu.SemaphoreType.DMA((3,)),
-            pltpu.SemaphoreType.DMA((5,)),
-            pltpu.SemaphoreType.DMA((SIDE,)),
             pltpu.SemaphoreType.DMA,
-            pltpu.SemaphoreType.DMA((13,)),
+            pltpu.SemaphoreType.DMA((17,)),
             pltpu.SemaphoreType.DMA((2,)),
         ],
         compiler_params=pltpu.CompilerParams(

time: 160 us -> 141 us (0.88)
  Pallas kernels: 156 us -> 137 us
    pallas_call x1, Pallas kernels: 69.8 us -> 57.6 us  [moe(): pl.pallas_call(functools.partial(moe_kernel, (n_dp, n_ep, chunks)), out_s...]
    pallas_call x1, Pallas kernels: 85.8 us -> 79.3 us  [attention(): pl.pallas_call(attention_kernel, out_shape=(jax.ShapeDtypeStruct((tokens,...]
where the time goes in v2:
time: 141 us
  Pallas kernels  137 us (97%)
  local copies, waits for them, and re-layouts  3.57 us (3%)
    pallas_call x1, Pallas kernels, attention(): pl.pallas_call(attention_kernel, out_shape=(jax.ShapeDtypeStruct((tokens,...  79.3 us
    pallas_call x1, Pallas kernels, moe(): pl.pallas_call(functools.partial(moe_kernel, (n_dp, n_ep, chunks)), out_s...  57.6 us

profile of v2, /device:TPU:1, one launch (start us, length us, event | category | flops | bytes accessed | tf_op | source)
XLA Modules:
  0.0 141.1 jit_solution(15212245718777159686)
XLA Ops:
  0.6 1.3 reshape.7.gain_ref
  1.9 79.3 %attention.1 = (f32[32,3584]{1,0:T(8,128)}, bf16[1,32,576]{2,1,0:T(8,128)(2,1)}) custom-call(s32[16]{0:T(128)} %lengths_ref.1, s32[16]{0:T(128)} %sources_ref.1, s32[16]{0:T(128)} %owner_ref.1, bf16[1,576,256]{2,1,0:T(8,128)(2,1)} %bitcast.7, bf16[1,32,576]{2,1,0:T(8,128)(2,1)} %new_ref.1, bf16[224,1024]{1,0:T(8,128)(2,1)} %bitcast.6, ...), custom_call_target="tpu_custom_call" | custom-call | tf_op jit(solution)/shard_map/attention/pallas_call | solution.py:685
  81.2 0.0 copy-start
  81.2 57.6 %experts.1 = bf16[32,3584]{1,0:T(8,128)(2,1)} custom-call(f32[32,3584]{1,0:T(8,128)} %get-tuple-element.4.att_ref, bf16[32,3584]{1,0:T(8,128)(2,1)} %res_ref.1, bf16[1,3584]{1,0:T(2,128)(2,1)} %reshape.7.gain_ref, s32[8,32]{1,0:T(8,128)} %bitcast.8, f32[8,32]{1,0:T(8,128)} %bitcast.9, bf16[1,3584,1024]{2,1,0:T(8,128)(2,1)} %gate_hbm.1, ...), custom_call_target="tpu_custom_call" | custom-call | tf_op jit(solution)/shard_map/experts/pallas_call | solution.py:226
  138.8 1.6 %copy.19 = bf16[32,3584]{1,0:T(8,128)(2,1)} copy(bf16[32,3584]{1,0:T(8,128)(2,1)} %experts.1) | data formatting | bytes 458752
  140.5 0.0 copy-done
  140.5 0.6 copy.20
Async XLA Ops:
  81.2 59.2 %copy-start = (bf16[1,32,576]{2,1,0:T(8,128)(2,1)S(1)}, bf16[1,32,576]{2,1,0:T(8,128)(2,1)}, u32[]{:S(2)}) copy-start(bf16[1,32,576]{2,1,0:T(8,128)(2,1)} %get-tuple-element.9) | copy-start | bytes 110596

commit v3 on v2

--- a/solution.py
+++ b/solution.py
@@ -168,7 +168,7 @@
 
     for c in range(chunks):
         span = pl.ds(c * cols, cols)
-        normed = (hid[:, span] * scale * gain_ref[:, span].astype(jnp.float32)).astype(
+        normed = (hid[:, span] * scale * gain_ref[span].astype(jnp.float32).reshape(1, cols)).astype(
             jnp.bfloat16
         )
         s1[c] = mm(picks[c % 2], normed).astype(jnp.bfloat16)
@@ -208,7 +208,7 @@
         wait_all(recv_sems, 3, c, q3)
         span = pl.ds(c * cols, cols)
         both = mm(weights[c % 2], q3[c])
-        out_ref[:, span] = (hid[:, span] + (both[:tokens] + both[tokens:])).astype(out_ref.dtype)
+        out_ref[:, span] = hid[:, span] + (both[:tokens] + both[tokens:])
     for stage, ref in enumerate((s1, s2, o1, q2)):
         for c in range(chunks):
             wait_all(send_sems, stage, c, ref)
@@ -225,7 +225,7 @@
     hbm = pl.BlockSpec(memory_space=pl.ANY)
     return pl.pallas_call(
         functools.partial(moe_kernel, (n_dp, n_ep, chunks)),
-        out_shape=jax.ShapeDtypeStruct((tokens, width), jnp.bfloat16),
+        out_shape=jax.ShapeDtypeStruct((tokens, width), jnp.float32),
         in_specs=[vmem] * 5 + [hbm] * 3,
         out_specs=vmem,
         scratch_shapes=[
@@ -254,7 +254,7 @@
     )(
         attention,
         residual,
-        norm_gain.reshape(1, -1),
+        norm_gain,
         expert_ids.T,
         gate_weights.T,
         expert_gate,
@@ -267,8 +267,7 @@
     return lax.dot_general(a, b, (((1,), (1,)), ((), ())), preferred_element_type=jnp.float32)
 
 
-def attend(q, keys, length, positions, prefix_len, lat):
-    s_old = contract_last(q, keys[0:prefix_len, :])
+def attend(q, s_old, keys, length, positions, prefix_len, lat):
     s_new = contract_last(q, keys[prefix_len:, :])
     old_pos = lax.broadcasted_iota(jnp.int32, (1, prefix_len), 1)
     s_old = s_old + jnp.where(old_pos < length, 0.0, -1e30)
@@ -307,6 +306,7 @@
     value_up,
     q_home,
     q_late,
+    scores,
     keys_own,
     late_own,
     late_in,
@@ -314,7 +314,6 @@
     rows_own,
     rows_in,
     rows_on,
-    rows_back,
     news_y,
     news_out,
     news_x,
@@ -470,6 +469,18 @@
     all_news = keys_own.at[pl.ds(0, (SIDE - 1) * new_part)]
     news_y[y] = new_ref[0]
     over_axis(False, lambda k: news_y.at[y], news_y.at[y], sends.at[3], dp_recv.at[1])
+
+    def score(k):
+        at = pl.ds(pl.multiple_of(around(z, k) * 2 * prefix_part, 2 * prefix_part), 2 * prefix_part)
+
+        def step(i, carry):
+            scores[i, :, at] = contract_last(q_home[i], keys_own[at])
+            return carry
+
+        lax.fori_loop(0, 4, step, 0)
+
+    wait(z_recv.at[6], key_full)
+    score(0)
     ring_forward(key_refs, right_z, left_z, sends.at[0], z_recv, key_half)
     wait(z_recv.at[1], key_half)
     share(-1, 7)
@@ -490,12 +501,16 @@
     )
     q_late[block_rows(dp, piece)] = late_on[dp]
     ring_start(proj_refs, right_y, left_y, sends.at[4], y_recv)
+    wait(z_recv.at[7], key_full)
+    score(-1)
+    wait(z_recv.at[8], key_full)
+    score(1)
     wait(z_recv.at[4], key_half)
     wait(z_recv.at[5], key_half)
     share(2, 9)
     load_v.wait()
-    for sem in range(6, 10):
-        wait(z_recv.at[sem], key_full)
+    wait(z_recv.at[9], key_full)
+    score(2)
 
     def given_to(slot):
         given = jnp.int32(0)
@@ -518,7 +533,10 @@
 
     def home_part(b, half):
         positions = home_pos + b * strip
-        out = attend(q_home[2 * b + half], keys_own, lengths_ref[dp], positions, prefix_len, lat)
+        i = 2 * b + half
+        out = attend(
+            q_home[i], scores[i], keys_own, lengths_ref[dp], positions, prefix_len, lat
+        )
         for j in range(quad):
             h = half * quad + j
             rows = jnp.dot(
@@ -591,7 +609,10 @@
     wait(dp_recv.at[2], all_late)
     late_row = lax.broadcasted_iota(jnp.int32, (head_count * late, 1), 0)
     late_pos = lax.rem(late_row, late) + home
-    out = attend(q_late[...], keys_own, lengths_ref[dp], late_pos, prefix_len, lat)
+    late_scores = contract_last(q_late[...], keys_own[0:prefix_len, :])
+    out = attend(
+        q_late[...], late_scores, keys_own, lengths_ref[dp], late_pos, prefix_len, lat
+    )
     for h in range(head_count):
         rows_own[pl.ds(h * late, late)] = jnp.dot(
             out[h * late : (h + 1) * late], value_up[h], preferred_element_type=jnp.float32
@@ -604,42 +625,41 @@
     wait(dp_recv.at[3], all_rows)
 
     def stage_rows(s, carry):
-        rows_on[s] = rows_in[sources_ref[s]]
+        at = pl.multiple_of((s // SIDE) * piece, piece)
+        rows_on[lax.rem(s, SIDE), pl.ds(at, piece)] = rows_in[sources_ref[s]]
         return carry
 
     lax.fori_loop(0, n_dp, stage_rows, 0)
+    quarter = SIDE * piece
+    landing = (
+        pl.ds(pl.multiple_of(lax.rem(dp, 2) * quarter, quarter), quarter),
+        pl.ds(pl.multiple_of((dp // 2) * vh, vh), vh),
+    )
     everywhere(
-        lambda p: rows_on.at[p], rows_back.at[block_rows(dp, piece)], sends.at[16], dp_recv.at[4]
-    )
-    rows_back[block_rows(dp, piece)] = rows_on[dp]
+        lambda p: rows_on.at[lax.rem(p, SIDE)],
+        heads_late.at[landing],
+        sends.at[16],
+        dp_recv.at[4],
+    )
+    heads_late[landing] = rows_on[y]
+    all_late_heads = heads_late.at[pl.ds(0, (n_dp - 1) * quarter * vh // heads_late.shape[1])]
     for i in (1, 2, 4, 5):
         wait(y_recv.at[i], proj_half)
     wait_heads(0)
     wait_heads(1)
     project(0, heads[0])
     home_part(1, 1)
-    wait(dp_recv.at[4], all_rows)
-    late_part = late // 2
-    refs = []
-    for c in range(2):
-        at = pl.multiple_of(c * SIDE * late_part + x * late_part, late_part)
-        refs.append(heads_late.at[pl.ds(at, late_part)])
-        for h in range(head_count):
-            heads_late[pl.ds(at, late_part), pl.ds(h * vh, vh)] = rows_back[
-                pl.ds(h * late + c * late_part, late_part)
-            ]
-    send_heads(4, refs)
     home_z = tuple(range(home // tokens // 2))
     late_z = (SIDE - 1,)
     home_rows, late_rows = SIDE * block, SIDE * late
     pass_on(0, home_rows, home_z, strip, 0)
+    wait(dp_recv.at[4], all_late_heads)
+    project(2, heads_late[...])
+    pass_on(2, late_rows, late_z, tokens, 0)
     wait_heads(2)
     wait_heads(3)
     project(1, heads[1])
-    wait(x_recv.at[4], heads_late.at[pl.ds(0, (SIDE - 1) * late)])
-    project(2, heads_late[...])
     pass_on(1, home_rows, home_z, strip, strip)
-    pass_on(2, late_rows, late_z, tokens, 0)
     wait(dp_recv.at[5], all_news)
     decode_ref[0] = news_x[given_to(dp) // SIDE]
     wait(last_recv, gathered.at[pl.ds(0, (n_dp - 1) * tokens)])
@@ -656,10 +676,9 @@
     wait(sends.at[15], all_news)
     wait(sends.at[4], proj.at[pl.ds(0, 3 * col_part)])
     wait(sends.at[5], all_rows)
-    wait(sends.at[16], all_rows)
+    wait(sends.at[16], all_late_heads)
     for i in range(4):
         wait(sends.at[6 + i], heads.at[0, pl.ds(0, (SIDE - 1) * block // 2)])
-    wait(sends.at[10], heads_late.at[pl.ds(0, (SIDE - 1) * late)])
     for i in range(2):
         wait(sends.at[11 + i], pair.at[i])
     wait(sends.at[13], pair.at[2, pl.ds(0, late_rows // 2)])
@@ -695,14 +714,14 @@
             pltpu.VMEM(value_up.shape, bf16),
             pltpu.VMEM((4, head_count // 2 * (home // 2), key_width), bf16),
             pltpu.VMEM((late_rows, key_width), bf16),
+            pltpu.VMEM((4, head_count // 2 * (home // 2), prefix_part * n_ep), f32),
             pltpu.VMEM((key_rows, key_width), bf16),
             pltpu.VMEM((late_rows, key_width), bf16),
             pltpu.VMEM((n_dp, late_rows // n_dp, key_width), bf16),
             pltpu.VMEM((n_dp, late_rows // n_dp, key_width), bf16),
             pltpu.VMEM((late_rows, vh), bf16),
             pltpu.VMEM((n_dp, late_rows // n_dp, vh), bf16),
-            pltpu.VMEM((n_dp, late_rows // n_dp, vh), bf16),
-            pltpu.VMEM((late_rows, vh), bf16),
+            pltpu.VMEM((SIDE, SIDE * late_rows // n_dp, vh), bf16),
             pltpu.VMEM((SIDE, new_part, key_width), bf16),
             pltpu.VMEM((SIDE, new_part, key_width), bf16),
             pltpu.VMEM((SIDE, new_part, key_width), bf16),
@@ -775,7 +794,7 @@
         expert_gate,
         expert_up,
         expert_down,
-    )
+    ).astype(jnp.bfloat16)
     return (layer_out, decode_latents)
 
 

time: 141 us -> 135 us (0.957)
  Pallas kernels: 137 us -> 132 us
  local copies, waits for them, and re-layouts: 3.57 us -> 0.62 us
  other arithmetic: 0 us -> 1.73 us
    pallas_call x1, Pallas kernels: 79.3 us -> 74.5 us  [attention(): pl.pallas_call(attention_kernel, out_shape=(jax.ShapeDtypeStruct((tokens,...]
    convert_element_type x0 -> x1, other arithmetic: none -> 1.73 us  [shards(): layer_out = moe(attention_sum, residual, norm_gain, expert_ids, gate_weig...]
    unnamed x4 -> x3, local copies, waits for them, and re-layouts: 2.26 us -> 0.62 us
where the time goes in v3:
time: 135 us
  Pallas kernels  132 us (98%)
  other arithmetic  1.73 us (1%)
    pallas_call x1, Pallas kernels, attention(): pl.pallas_call(attention_kernel, out_shape=(jax.ShapeDtypeStruct((tokens,...  74.5 us
    pallas_call x1, Pallas kernels, moe(): pl.pallas_call(functools.partial(moe_kernel, (n_dp, n_ep, chunks)), out_s...  57.3 us

profile of v3, /device:TPU:1, one launch (start us, length us, event | category | flops | bytes accessed | tf_op | source)
XLA Modules:
  0.0 134.8 jit_solution(2488628654948065576)
XLA Ops:
  0.6 74.5 %attention.1 = (f32[32,3584]{1,0:T(8,128)}, bf16[1,32,576]{2,1,0:T(8,128)(2,1)}) custom-call(s32[16]{0:T(128)} %lengths_ref.1, s32[16]{0:T(128)} %sources_ref.1, s32[16]{0:T(128)} %owner_ref.1, bf16[1,576,256]{2,1,0:T(8,128)(2,1)} %bitcast.7, bf16[1,32,576]{2,1,0:T(8,128)(2,1)} %new_ref.1, bf16[224,1024]{1,0:T(8,128)(2,1)} %bitcast.6, ...), custom_call_target="tpu_custom_call" | custom-call | tf_op jit(solution)/shard_map/attention/pallas_call | solution.py:704
  75.1 0.0 copy-start
  75.1 57.3 %experts.1 = f32[32,3584]{1,0:T(8,128)} custom-call(f32[32,3584]{1,0:T(8,128)} %get-tuple-element.4.att_ref, bf16[32,3584]{1,0:T(8,128)(2,1)} %res_ref.1, bf16[3584]{0:T(1024)(128)(2,1)} %gain_ref.1, s32[8,32]{1,0:T(8,128)} %bitcast.8, f32[8,32]{1,0:T(8,128)} %bitcast.9, bf16[1,3584,1024]{2,1,0:T(8,128)(2,1)} %gate_hbm.1, bf16[1,3584,1024]{2,1,0:T(8,128)(2,1)} %up_hbm.1, ...), custom_call_target="tpu_custom_call" | custom-call | tf_op jit(solution)/shard_map/experts/pallas_call | solution.py:226
  132.4 1.7 %convert_element_type.3 = bf16[32,3584]{1,0:T(8,128)(2,1)} convert(f32[32,3584]{1,0:T(8,128)} %experts.1) | non-fusion elementwise | flops 114688 | bytes 688128 | tf_op jit(solution)/shard_map/convert_element_type | solution.py:797
  134.2 0.0 copy-done
  134.2 0.6 copy.18
Async XLA Ops:
  75.1 59.1 %copy-start = (bf16[1,32,576]{2,1,0:T(8,128)(2,1)S(1)}, bf16[1,32,576]{2,1,0:T(8,128)(2,1)}, u32[]{:S(2)}) copy-start(bf16[1,32,576]{2,1,0:T(8,128)(2,1)} %get-tuple-element.9) | copy-start | bytes 110596

commit v4 on v3

--- a/solution.py
+++ b/solution.py
@@ -72,9 +72,6 @@
         pltpu.make_async_copy(src.at[0], dst, weight_sems.at[i])
         for i, (src, dst) in enumerate(((gate_hbm, w_gate), (up_hbm, w_up), (down_hbm, w_down)))
     ]
-    for load in loads:
-        load.start()
-
     barrier = pltpu.get_barrier_semaphore()
     partners(
         n_dp,
@@ -173,10 +170,13 @@
         )
         s1[c] = mm(picks[c % 2], normed).astype(jnp.bfloat16)
         hop(0, c, s1, r1)
+    loads[0].start()
+    loads[1].start()
     for c in range(chunks):
         wait_all(recv_sems, 0, c, r1)
         s2[c] = mm(perms[c % 2], r1[c]).astype(jnp.bfloat16)
         hop(1, c, s2, r2)
+    loads[2].start()
     loads[0].wait()
     loads[1].wait()
     for c in range(chunks):

time: 135 us -> 135 us (level)
  no operation moved by 1% of the time
where the time goes in v4:
time: 135 us
  Pallas kernels  132 us (98%)
  other arithmetic  1.73 us (1%)
    pallas_call x1, Pallas kernels, attention(): pl.pallas_call(attention_kernel, out_shape=(jax.ShapeDtypeStruct((tokens,...  74.5 us
    pallas_call x1, Pallas kernels, moe(): pl.pallas_call(functools.partial(moe_kernel, (n_dp, n_ep, chunks)), out_s...  57.4 us

profile of v4, /device:TPU:1, one launch (start us, length us, event | category | flops | bytes accessed | tf_op | source)
XLA Modules:
  0.0 134.9 jit_solution(9000426324314862600)
XLA Ops:
  0.6 74.5 %attention.1 = (f32[32,3584]{1,0:T(8,128)}, bf16[1,32,576]{2,1,0:T(8,128)(2,1)}) custom-call(s32[16]{0:T(128)} %lengths_ref.1, s32[16]{0:T(128)} %sources_ref.1, s32[16]{0:T(128)} %owner_ref.1, bf16[1,576,256]{2,1,0:T(8,128)(2,1)} %bitcast.7, bf16[1,32,576]{2,1,0:T(8,128)(2,1)} %new_ref.1, bf16[224,1024]{1,0:T(8,128)(2,1)} %bitcast.6, ...), custom_call_target="tpu_custom_call" | custom-call | tf_op jit(solution)/shard_map/attention/pallas_call | solution.py:704
  75.1 0.0 copy-start
  75.1 57.4 %experts.1 = f32[32,3584]{1,0:T(8,128)} custom-call(f32[32,3584]{1,0:T(8,128)} %get-tuple-element.4.att_ref, bf16[32,3584]{1,0:T(8,128)(2,1)} %res_ref.1, bf16[3584]{0:T(1024)(128)(2,1)} %gain_ref.1, s32[8,32]{1,0:T(8,128)} %bitcast.8, f32[8,32]{1,0:T(8,128)} %bitcast.9, bf16[1,3584,1024]{2,1,0:T(8,128)(2,1)} %gate_hbm.1, bf16[1,3584,1024]{2,1,0:T(8,128)(2,1)} %up_hbm.1, ...), custom_call_target="tpu_custom_call" | custom-call | tf_op jit(solution)/shard_map/experts/pallas_call | solution.py:226
  132.5 1.7 %convert_element_type.3 = bf16[32,3584]{1,0:T(8,128)(2,1)} convert(f32[32,3584]{1,0:T(8,128)} %experts.1) | non-fusion elementwise | flops 114688 | bytes 688128 | tf_op jit(solution)/shard_map/convert_element_type | solution.py:797
  134.3 0.0 copy-done
  134.3 0.6 copy.18
Async XLA Ops:
  75.1 59.2 %copy-start = (bf16[1,32,576]{2,1,0:T(8,128)(2,1)S(1)}, bf16[1,32,576]{2,1,0:T(8,128)(2,1)}, u32[]{:S(2)}) copy-start(bf16[1,32,576]{2,1,0:T(8,128)(2,1)} %get-tuple-element.9) | copy-start | bytes 110596

commit v5 on v3

--- a/solution.py
+++ b/solution.py
@@ -648,11 +648,11 @@
     wait_heads(0)
     wait_heads(1)
     project(0, heads[0])
-    home_part(1, 1)
     home_z = tuple(range(home // tokens // 2))
     late_z = (SIDE - 1,)
     home_rows, late_rows = SIDE * block, SIDE * late
     pass_on(0, home_rows, home_z, strip, 0)
+    home_part(1, 1)
     wait(dp_recv.at[4], all_late_heads)
     project(2, heads_late[...])
     pass_on(2, late_rows, late_z, tokens, 0)

time: 135 us -> 137 us (1.015)
  Pallas kernels: 132 us -> 134 us
    pallas_call x1, Pallas kernels: 74.5 us -> 76.3 us  [attention(): pl.pallas_call(attention_kernel, out_shape=(jax.ShapeDtypeStruct((tokens,...]
where the time goes in v5:
time: 137 us
  Pallas kernels  134 us (98%)
  other arithmetic  1.73 us (1%)
    pallas_call x1, Pallas kernels, attention(): pl.pallas_call(attention_kernel, out_shape=(jax.ShapeDtypeStruct((tokens,...  76.3 us
    pallas_call x1, Pallas kernels, moe(): pl.pallas_call(functools.partial(moe_kernel, (n_dp, n_ep, chunks)), out_s...  57.7 us

profile of v5, /device:TPU:1, one launch (start us, length us, event | category | flops | bytes accessed | tf_op | source)
XLA Modules:
  0.0 136.9 jit_solution(711147241316804697)
XLA Ops:
  0.6 76.3 %attention.1 = (f32[32,3584]{1,0:T(8,128)}, bf16[1,32,576]{2,1,0:T(8,128)(2,1)}) custom-call(s32[16]{0:T(128)} %lengths_ref.1, s32[16]{0:T(128)} %sources_ref.1, s32[16]{0:T(128)} %owner_ref.1, bf16[1,576,256]{2,1,0:T(8,128)(2,1)} %bitcast.7, bf16[1,32,576]{2,1,0:T(8,128)(2,1)} %new_ref.1, bf16[224,1024]{1,0:T(8,128)(2,1)} %bitcast.6, ...), custom_call_target="tpu_custom_call" | custom-call | tf_op jit(solution)/shard_map/attention/pallas_call | solution.py:704
  76.9 0.0 copy-start
  76.9 57.7 %experts.1 = f32[32,3584]{1,0:T(8,128)} custom-call(f32[32,3584]{1,0:T(8,128)} %get-tuple-element.4.att_ref, bf16[32,3584]{1,0:T(8,128)(2,1)} %res_ref.1, bf16[3584]{0:T(1024)(128)(2,1)} %gain_ref.1, s32[8,32]{1,0:T(8,128)} %bitcast.8, f32[8,32]{1,0:T(8,128)} %bitcast.9, bf16[1,3584,1024]{2,1,0:T(8,128)(2,1)} %gate_hbm.1, bf16[1,3584,1024]{2,1,0:T(8,128)(2,1)} %up_hbm.1, ...), custom_call_target="tpu_custom_call" | custom-call | tf_op jit(solution)/shard_map/experts/pallas_call | solution.py:226
  134.6 1.7 %convert_element_type.3 = bf16[32,3584]{1,0:T(8,128)(2,1)} convert(f32[32,3584]{1,0:T(8,128)} %experts.1) | non-fusion elementwise | flops 114688 | bytes 688128 | tf_op jit(solution)/shard_map/convert_element_type | solution.py:797
  136.3 0.0 copy-done
  136.3 0.6 copy.18
Async XLA Ops:
  76.9 59.4 %copy-start = (bf16[1,32,576]{2,1,0:T(8,128)(2,1)S(1)}, bf16[1,32,576]{2,1,0:T(8,128)(2,1)}, u32[]{:S(2)}) copy-start(bf16[1,32,576]{2,1,0:T(8,128)(2,1)} %get-tuple-element.9) | copy-start | bytes 110596
